TPU v7x, 32 devices: a whole 2x2x4 slice. The times are simulated.
32 devices in a mesh: ctx: 8 (over y, x, core), fsdp: 4 (over z).
Axes of the slice: x: 2, y: 2, z: 4, core: 2. Of those that a mesh axis runs over, the one named last changes fastest.
Arguments:
- tokens: bfloat16 [4, 1024, 768], P('fsdp', 'ctx'), may hold values from -6 to 6
- cotangent: bfloat16 [4, 1024, 768], P('fsdp', 'ctx'), may hold values from -6 to 6
- att_gain: bfloat16 [768], P('fsdp'), may hold values from 0.25 to 1.75
- att_shift: bfloat16 [768], P('fsdp'), may hold values from -1.75 to 1.75
- ffn_gain: bfloat16 [768], P('fsdp'), may hold values from 0.25 to 1.75
- ffn_shift: bfloat16 [768], P('fsdp'), may hold values from -1.75 to 1.75
- qkv_weight: bfloat16 [768, 2304], P('fsdp'), may hold values from -0.3125 to 0.3125
- qkv_bias: bfloat16 [2304], P('fsdp'), may hold values from -3 to 3
- out_weight: bfloat16 [768, 768], P('fsdp'), may hold values from -0.875 to 0.875
- out_bias: bfloat16 [768], P('fsdp'), may hold values from -3 to 3
- up_weight: bfloat16 [768, 3072], P(None, 'fsdp'), may hold values from -0.21875 to 0.21875
- up_bias: bfloat16 [3072], P('fsdp'), may hold values from -3 to 3
- down_weight: bfloat16 [3072, 768], P('fsdp'), may hold values from -0.109375 to 0.109375
- down_bias: bfloat16 [768], P('fsdp'), may hold values from -3 to 3
Outputs:
- layer_out: bfloat16 [4, 1024, 768], P('fsdp', 'ctx')
- input_grad: float32 [4, 1024, 768], P('fsdp', 'ctx')
- att_dgain: float32 [768], P('fsdp')
- att_dshift: float32 [768], P('fsdp')
- ffn_dgain: float32 [768], P('fsdp')
- ffn_dshift: float32 [768], P('fsdp')
- qkv_dweight: float32 [768, 2304], P('fsdp')
- qkv_dbias: float32 [2304], P('fsdp')
- out_dweight: float32 [768, 768], P('fsdp')
- out_dbias: float32 [768], P('fsdp')
- up_dweight: float32 [768, 3072], P(None, 'fsdp')
- up_dbias: float32 [3072], P('fsdp')
- down_dweight: float32 [3072, 768], P('fsdp')
- down_dbias: float32 [768], P('fsdp')
All inputs are finite; a program needn't handle non-finite values.
Results may differ from a plain program's by a relative error of at most 0.012.
The roundings to bfloat16 on the way count: a program that leaves them out, or rounds other values in their place, can miss the bound.
Values may be sent and summed in bfloat16 or wider, within the bound.
No kernel may reach another device: no remote copies, remote signals or barrier semaphores. Data moves between devices by JAX's collectives and lax.ppermute only.
A program may use at most 192 MiB of HBM per device.

v0:
```python
import math

import jax
import jax.numpy as jnp
from jax import lax
from jax.sharding import PartitionSpec as P

HEADS = 12
HEAD_DIM = 64
ROT_DIMS = 16


def layer_norm(values, norm_gain, norm_shift):
    center = values - jnp.mean(values, axis=-1, keepdims=True)
    spread = jnp.mean(center * center, axis=-1, keepdims=True)
    return center * lax.rsqrt(spread + 1e-05) * norm_gain + norm_shift


def exact_gelu(values):
    return jax.nn.gelu(values, approximate=False)


def stored_positions(rows, devices):
    row_order = jnp.arange(rows * devices, dtype=jnp.int32)
    device = row_order // rows
    within = row_order % rows
    half_rows = rows // 2
    return jnp.where(
        within < half_rows,
        device * half_rows + within,
        (2 * devices - 1 - device) * half_rows + within - half_rows,
    )


def rotary_angles(positions):
    half_rot = ROT_DIMS // 2
    inverse = jnp.power(10000.0, -2.0 * jnp.arange(half_rot, dtype=jnp.float32) / ROT_DIMS)
    return positions.astype(jnp.float32)[:, None] * inverse[None, :]


def rotate(heads, angles):
    half_rot = ROT_DIMS // 2
    cosine = jnp.cos(angles)[:, None, :]
    sine_part = jnp.sin(angles)[:, None, :]
    lower_half = heads[..., :half_rot]
    upper_half = heads[..., half_rot:ROT_DIMS]
    return jnp.concatenate(
        [
            lower_half * cosine - upper_half * sine_part,
            upper_half * cosine + lower_half * sine_part,
            heads[..., ROT_DIMS:],
        ],
        axis=-1,
    )


def to_order(stack, ctx_count, half_rows):
    tail = stack.shape[1:]
    shaped = stack.reshape((ctx_count, 2, half_rows) + tail)
    return jnp.concatenate(
        [shaped[:, 0].reshape((-1,) + tail), shaped[::-1, 1].reshape((-1,) + tail)], axis=0
    )


def from_order(stack, ctx_count, half_rows):
    tail = stack.shape[1:]
    middle = stack.shape[0] // 2
    first = stack[:middle].reshape((ctx_count, half_rows) + tail)
    second = stack[middle:].reshape((ctx_count, half_rows) + tail)[::-1]
    return jnp.stack([first, second], axis=1).reshape(stack.shape)


def scores_block(query_heads, key_heads, query_pos, key_pos):
    scores = jnp.einsum(
        "qhd,khd->hqk", query_heads, key_heads, preferred_element_type=jnp.float32
    ) / math.sqrt(HEAD_DIM)
    return jnp.where(key_pos[None, None, :] <= query_pos[None, :, None], scores, -1000000000.0)


def grad_block(
    query_heads, grad_heads, log_total, inner, query_pos, key_heads, value_heads, key_pos
):
    scores = scores_block(query_heads, key_heads, query_pos, key_pos)
    probability = jnp.exp(scores - log_total[:, :, None])
    prob_grad = jnp.einsum(
        "qhd,khd->hqk", grad_heads, value_heads, preferred_element_type=jnp.float32
    )
    score_grad = (probability * (prob_grad - inner[:, :, None])).astype(jnp.bfloat16)
    return (probability.astype(jnp.bfloat16), score_grad)


def shards(
    tokens,
    cotangent,
    att_gain,
    att_shift,
    ffn_gain,
    ffn_shift,
    qkv_weight,
    qkv_bias,
    out_weight,
    out_bias,
    up_weight,
    up_bias,
    down_weight,
    down_bias,
):
    model_width = tokens.shape[-1]
    rows_in = tokens.reshape(-1, model_width)
    grad_rows = cotangent.reshape(-1, model_width)
    own_rows = rows_in.shape[0]
    half_rows = own_rows // 2
    ctx_count = lax.axis_size("ctx")
    ctx_place = lax.axis_index("ctx")
    total_rows = own_rows * ctx_count
    all_pos = stored_positions(own_rows, ctx_count)
    own_pos = lax.dynamic_slice_in_dim(all_pos, ctx_place * own_rows, own_rows, 0)
    (
        gain_attend,
        shift_attend,
        gain_feed,
        shift_feed,
        mat_qkv,
        bias_qkv,
        mat_out,
        bias_out,
        bias_down,
    ) = (
        lax.all_gather(att_gain, "fsdp", axis=0, tiled=True),
        lax.all_gather(att_shift, "fsdp", axis=0, tiled=True),
        lax.all_gather(ffn_gain, "fsdp", axis=0, tiled=True),
        lax.all_gather(ffn_shift, "fsdp", axis=0, tiled=True),
        lax.all_gather(qkv_weight, "fsdp", axis=0, tiled=True),
        lax.all_gather(qkv_bias, "fsdp", axis=0, tiled=True),
        lax.all_gather(out_weight, "fsdp", axis=0, tiled=True),
        lax.all_gather(out_bias, "fsdp", axis=0, tiled=True),
        lax.all_gather(down_bias, "fsdp", axis=0, tiled=True),
    )
    tokens32 = rows_in.astype(jnp.float32)
    grad32 = grad_rows.astype(jnp.float32)
    first_norm, first_back = jax.vjp(
        layer_norm, tokens32, gain_attend.astype(jnp.float32), shift_attend.astype(jnp.float32)
    )
    second_norm, second_back = jax.vjp(
        layer_norm, tokens32, gain_feed.astype(jnp.float32), shift_feed.astype(jnp.float32)
    )
    first_in = first_norm.astype(jnp.bfloat16)
    second_in = second_norm.astype(jnp.bfloat16)
    joined = jnp.dot(first_in, mat_qkv, preferred_element_type=jnp.float32) + bias_qkv.astype(
        jnp.float32
    )
    angles = rotary_angles(own_pos)

    def project_heads(joined_rows):
        queries = rotate(joined_rows[:, :model_width].reshape(own_rows, HEADS, HEAD_DIM), angles)
        keys_rot = rotate(
            joined_rows[:, model_width : 2 * model_width].reshape(own_rows, HEADS, HEAD_DIM), angles
        )
        return (
            queries.reshape(own_rows, model_width),
            keys_rot.reshape(own_rows, model_width),
            joined_rows[:, 2 * model_width :],
        )

    (queries, keys_rot, values_rows), rotary_back = jax.vjp(project_heads, joined)
    query_low = queries.astype(jnp.bfloat16)
    key_low = keys_rot.astype(jnp.bfloat16)
    value_low = values_rows.astype(jnp.bfloat16)
    key_all, value_all = (
        lax.all_gather(key_low, "ctx", axis=0, tiled=True),
        lax.all_gather(value_low, "ctx", axis=0, tiled=True),
    )
    query_heads = query_low.reshape(own_rows, HEADS, HEAD_DIM)
    key_heads = to_order(key_all, ctx_count, half_rows).reshape(total_rows, HEADS, HEAD_DIM)
    value_heads = to_order(value_all, ctx_count, half_rows).reshape(total_rows, HEADS, HEAD_DIM)
    block_keys = min(1024, total_rows)

    def key_piece(block_index):
        start = block_index * block_keys
        return (
            lax.dynamic_slice_in_dim(key_heads, start, block_keys, 0),
            lax.dynamic_slice_in_dim(value_heads, start, block_keys, 0),
            start + jnp.arange(block_keys, dtype=jnp.int32),
        )

    need_low = (ctx_place + 1) * half_rows
    need_high = (2 * ctx_count - ctx_place) * half_rows
    counts = ((need_low + block_keys - 1) // block_keys, (need_high + block_keys - 1) // block_keys)
    query_parts = (query_heads[:half_rows], query_heads[half_rows:])
    pos_parts = (own_pos[:half_rows], own_pos[half_rows:])

    def half_lse(query_half, pos_half, count):

        def lse_step(block_index, carried):
            row_top, exp_total = carried
            key_block, value_skip, key_pos = key_piece(block_index)
            scores = scores_block(query_half, key_block, pos_half, key_pos)
            new_top = jnp.maximum(row_top, jnp.max(scores, axis=-1))
            exp_total = exp_total * jnp.exp(row_top - new_top) + jnp.sum(
                jnp.exp(scores - new_top[:, :, None]), axis=-1
            )
            return (new_top, exp_total)

        start_top = jnp.full((HEADS, half_rows), -1e30, jnp.float32)
        start_sum = jnp.zeros((HEADS, half_rows), jnp.float32)
        row_top, exp_total = lax.fori_loop(0, count, lse_step, (start_top, start_sum))
        return row_top + jnp.log(exp_total)

    lse_parts = [
        half_lse(query_parts[half_index], pos_parts[half_index], counts[half_index])
        for half_index in range(2)
    ]

    def half_mix(query_half, pos_half, lse_half, count):

        def mix_step(block_index, totals):
            key_block, value_block, key_pos = key_piece(block_index)
            scores = scores_block(query_half, key_block, pos_half, key_pos)
            probability = jnp.exp(scores - lse_half[:, :, None]).astype(jnp.bfloat16)
            return totals + jnp.einsum(
                "hqk,khd->qhd", probability, value_block, preferred_element_type=jnp.float32
            )

        return lax.fori_loop(
            0, count, mix_step, jnp.zeros((half_rows, HEADS, HEAD_DIM), jnp.float32)
        )

    attended = jnp.concatenate(
        [
            half_mix(
                query_parts[half_index],
                pos_parts[half_index],
                lse_parts[half_index],
                counts[half_index],
            )
            for half_index in range(2)
        ],
        axis=0,
    )
    attended_low = attended.reshape(own_rows, model_width).astype(jnp.bfloat16)
    branch_att = jnp.dot(
        attended_low, mat_out, preferred_element_type=jnp.float32
    ) + bias_out.astype(jnp.float32)
    second_all, grad_all = (
        lax.all_gather(second_in, "fsdp", axis=0, tiled=True),
        lax.all_gather(grad_rows, "fsdp", axis=0, tiled=True),
    )
    hidden = jnp.dot(second_all, up_weight, preferred_element_type=jnp.float32) + up_bias.astype(
        jnp.float32
    )
    active, gelu_back = jax.vjp(exact_gelu, hidden)
    active_low = active.astype(jnp.bfloat16)
    ffn_part = jnp.dot(active_low, down_weight, preferred_element_type=jnp.float32)
    active_grad = jnp.einsum("te,fe->tf", grad_all, down_weight, preferred_element_type=jnp.float32)
    hidden_grad = gelu_back(active_grad)[0].astype(jnp.bfloat16)
    down_dweight = jnp.einsum("tf,te->fe", active_low, grad_all, preferred_element_type=jnp.float32)
    up_dweight = jnp.einsum(
        "td,tf->df", second_all, hidden_grad, preferred_element_type=jnp.float32
    )
    up_dbias = jnp.sum(hidden_grad.astype(jnp.float32), axis=0)
    second_part = jnp.einsum(
        "tf,df->td", hidden_grad, up_weight, preferred_element_type=jnp.float32
    )
    ffn_sum, second_grad = (
        lax.psum_scatter(ffn_part, "fsdp", scatter_dimension=0, tiled=True),
        lax.psum_scatter(second_part, "fsdp", scatter_dimension=0, tiled=True),
    )
    branch_ffn = ffn_sum + bias_down.astype(jnp.float32)
    layer_out = (tokens32 + branch_att + branch_ffn).astype(jnp.bfloat16).reshape(tokens.shape)
    out_dweight = jnp.einsum(
        "td,te->de", attended_low, grad_rows, preferred_element_type=jnp.float32
    )
    row_sum = jnp.sum(grad32, axis=0)
    attended_grad = jnp.einsum(
        "te,de->td", grad_rows, mat_out, preferred_element_type=jnp.float32
    ).astype(jnp.bfloat16)
    grad_heads = attended_grad.reshape(own_rows, HEADS, HEAD_DIM)
    grad_parts = (grad_heads[:half_rows], grad_heads[half_rows:])

    def half_inner(query_half, grad_half, pos_half, lse_half, count):

        def inner_step(block_index, totals):
            key_block, value_block, key_pos = key_piece(block_index)
            scores = scores_block(query_half, key_block, pos_half, key_pos)
            probability = jnp.exp(scores - lse_half[:, :, None])
            prob_grad = jnp.einsum(
                "qhd,khd->hqk", grad_half, value_block, preferred_element_type=jnp.float32
            )
            return totals + jnp.sum(probability * prob_grad, axis=-1)

        return lax.fori_loop(0, count, inner_step, jnp.zeros((HEADS, half_rows), jnp.float32))

    inner_parts = [
        half_inner(
            query_parts[half_index],
            grad_parts[half_index],
            pos_parts[half_index],
            lse_parts[half_index],
            counts[half_index],
        )
        for half_index in range(2)
    ]
    half_zeros = jnp.zeros((half_rows, HEADS, HEAD_DIM), jnp.float32)

    def half_back(half_index, carried):
        query_half = query_parts[half_index]
        grad_half = grad_parts[half_index]

        def query_step(block_index, state):
            query_total, key_acc, value_acc = state
            key_block, value_block, key_pos = key_piece(block_index)
            prob_low, score_grad = grad_block(
                query_half,
                grad_half,
                lse_parts[half_index],
                inner_parts[half_index],
                pos_parts[half_index],
                key_block,
                value_block,
                key_pos,
            )
            key_part = jnp.einsum(
                "hqk,qhd->khd", score_grad, query_half, preferred_element_type=jnp.float32
            )
            value_part = jnp.einsum(
                "hqk,qhd->khd", prob_low, grad_half, preferred_element_type=jnp.float32
            )
            start = block_index * block_keys
            key_acc = lax.dynamic_update_slice_in_dim(
                key_acc,
                lax.dynamic_slice_in_dim(key_acc, start, block_keys, 0) + key_part,
                start,
                0,
            )
            value_acc = lax.dynamic_update_slice_in_dim(
                value_acc,
                lax.dynamic_slice_in_dim(value_acc, start, block_keys, 0) + value_part,
                start,
                0,
            )
            query_total = query_total + jnp.einsum(
                "hqk,khd->qhd", score_grad, key_block, preferred_element_type=jnp.float32
            )
            return (query_total, key_acc, value_acc)

        return lax.fori_loop(0, counts[half_index], query_step, carried)

    full_zeros = jnp.zeros((total_rows, HEADS, HEAD_DIM), jnp.float32)
    query_low_sum, key_acc, value_acc = half_back(0, (half_zeros, full_zeros, full_zeros))
    query_high_sum, key_acc, value_acc = half_back(1, (half_zeros, key_acc, value_acc))
    query_sum = jnp.concatenate([query_low_sum, query_high_sum], axis=0)
    key_stored = from_order(key_acc.reshape(total_rows, model_width), ctx_count, half_rows)
    value_stored = from_order(value_acc.reshape(total_rows, model_width), ctx_count, half_rows)
    key_sum, value_sum = (
        lax.psum_scatter(key_stored, "ctx", scatter_dimension=0, tiled=True),
        lax.psum_scatter(value_stored, "ctx", scatter_dimension=0, tiled=True),
    )
    query_grad = query_sum.reshape(own_rows, model_width) / math.sqrt(HEAD_DIM)
    key_grad = key_sum / math.sqrt(HEAD_DIM)
    joined_grad = rotary_back((query_grad, key_grad, value_sum))[0].astype(jnp.bfloat16)
    qkv_dweight = jnp.einsum("td,tf->df", first_in, joined_grad, preferred_element_type=jnp.float32)
    qkv_dbias = jnp.sum(joined_grad.astype(jnp.float32), axis=0)
    first_grad = jnp.einsum("tf,df->td", joined_grad, mat_qkv, preferred_element_type=jnp.float32)
    token_first, att_dgain, att_dshift = first_back(first_grad)
    token_second, ffn_dgain, ffn_dshift = second_back(second_grad)
    input_grad = (grad32 + token_first + token_second).reshape(tokens.shape)
    shares = (
        lax.psum_scatter(att_dgain, "fsdp", scatter_dimension=0, tiled=True),
        lax.psum_scatter(att_dshift, "fsdp", scatter_dimension=0, tiled=True),
        lax.psum_scatter(ffn_dgain, "fsdp", scatter_dimension=0, tiled=True),
        lax.psum_scatter(ffn_dshift, "fsdp", scatter_dimension=0, tiled=True),
        lax.psum_scatter(qkv_dweight, "fsdp", scatter_dimension=0, tiled=True),
        lax.psum_scatter(qkv_dbias, "fsdp", scatter_dimension=0, tiled=True),
        lax.psum_scatter(out_dweight, "fsdp", scatter_dimension=0, tiled=True),
        lax.psum_scatter(row_sum, "fsdp", scatter_dimension=0, tiled=True),
    ) + (up_dweight, up_dbias, down_dweight)
    totals = lax.psum(
        (
            shares[0],
            shares[1],
            shares[2],
            shares[3],
            shares[4],
            shares[5],
            shares[6],
            shares[7],
            shares[8],
            shares[9],
            shares[10],
        ),
        "ctx",
    )
    return (
        layer_out,
        input_grad,
        totals[0],
        totals[1],
        totals[2],
        totals[3],
        totals[4],
        totals[5],
        totals[6],
        totals[7],
        totals[8],
        totals[9],
        totals[10],
        totals[7],
    )


def solution(mesh):
    in_specs = (
        P("fsdp", "ctx", None),
        P("fsdp", "ctx", None),
        P("fsdp"),
        P("fsdp"),
        P("fsdp"),
        P("fsdp"),
        P("fsdp", None),
        P("fsdp"),
        P("fsdp", None),
        P("fsdp"),
        P(None, "fsdp"),
        P("fsdp"),
        P("fsdp", None),
        P("fsdp"),
    )
    out_specs = (
        P("fsdp", "ctx", None),
        P("fsdp", "ctx", None),
        P("fsdp"),
        P("fsdp"),
        P("fsdp"),
        P("fsdp"),
        P("fsdp", None),
        P("fsdp"),
        P("fsdp", None),
        P("fsdp"),
        P(None, "fsdp"),
        P("fsdp"),
        P("fsdp", None),
        P("fsdp"),
    )
    return jax.shard_map(shards, mesh=mesh, in_specs=in_specs, out_specs=out_specs, check_vma=False)
```

profile of v0, /device:TPU:0, one launch (start us, length us, event | category | flops | bytes accessed | tf_op | source)
XLA Modules:
  0.0 779.1 jit_solution(2651655638125433972)
XLA Ops:
  18.4 22.4 %all-reduce.25 = (bf16[2304]{0:T(1024)(128)(2,1)S(1)}, bf16[768]{0:T(1024)(128)(2,1)S(1)}, bf16[768]{0:T(1024)(128)(2,1)S(1)}, bf16[768]{0:T(1024)(128)(2,1)}, b...) all-reduce(bf16[2304]{0:T(1024)(128)(2,1)S(1)} %dynamic-update-slic, ...), channel_id=1, replica_groups=mesh['ctx'=8,'fsdp'=4] {'fsdp'}, use_global_device_ids=true, to_apply=%add.11 | all-reduce | flops 6912 | bytes 27648
  41.2 42.2 %all-gather.6.cloned.1.call-done = bf16[768,2304]{1,0:T(8,128)(2,1)} async-done(((bf16[192,2304]{1,0:T(8,128)(2,1)}), bf16[768,2304]{1,0:T(8,128)(2,1)}) %all-gather.6.cloned.1.call-update) | async-done | bytes 3538960 | tf_op jit(solution)/shard_map/all_gather | solution.py:133
  90.6 23.3 %all-gather.12.cloned.1.call-done = bf16[768,768]{1,0:T(8,128)(2,1)} async-done(((bf16[192,768]{1,0:T(8,128)(2,1)}), bf16[768,768]{1,0:T(8,128)(2,1)}) %all-gather.12.cloned.1.call-update) | async-done | bytes 1179664 | tf_op jit(solution)/shard_map/all_gather | solution.py:135
  120.6 20.8 %all-gather.8.cloned.1.call-done = bf16[1024,768]{0,1:T(8,128)(2,1)} async-done(((bf16[128,768]{0,1:T(8,128)(2,1)}), bf16[1024,768]{0,1:T(8,128)(2,1)}) %all-gather.8.cloned.1.call-update) | async-done | bytes 1572880 | tf_op jit(solution)/shard_map/all_gather | solution.py:170
  154.2 3.5 concatenate.42
  161.3 8.1 %all-gather.10.cloned.1.call-done = bf16[1024,768]{1,0:T(8,128)(2,1)} async-done(((bf16[128,768]{1,0:T(8,128)(2,1)}), bf16[1024,768]{1,0:T(8,128)(2,1)}) %all-gather.10.cloned.1.call-update) | async-done | bytes 1572880 | tf_op jit(solution)/shard_map/all_gather | solution.py:171
  174.9 4.6 rev.13
  179.5 3.4 concatenate.45
  185.7 3.5 concatenate.44
  192.4 6.9 while.98
  195.6 3.6 multiply_reduce_fusion.5
  203.6 6.0 while.96
  206.0 3.7 multiply_reduce_fusion.4
  214.6 16.4 %while.97 = (s32[]{:T(128)}, f32[64,12,64]{2,0,1:T(8,128)}, f32[1024,12,64]{0,2,1:T(8,128)}, f32[1024,12,64]{0,2,1:T(8,128)}, s32[]{:T(128)}, /*index=5*/s32[64]...) while((s32[]{:T(128)}, f32[64,12,64]{2,0,1:T(8,128)}, ...), condition=%wide.region_19.20_spmd, body=%wide.region_18.19_spmd.sunk | while | flops 512869376 | bytes 72185432 | solution.py:346
  217.6 3.9 multiply_convert_fusion.5
  226.2 4.8 bitcast_add_fusion.9
  231.8 16.2 %while.99 = (s32[]{:T(128)}, f32[64,12,64]{2,0,1:T(8,128)}, f32[1024,12,64]{0,2,1:T(8,128)}, f32[1024,12,64]{0,2,1:T(8,128)}, s32[]{:T(128)}, /*index=5*/s32[64]...) while((s32[]{:T(128)}, f32[64,12,64]{2,0,1:T(8,128)}, ...), condition=%wide.region_24.25_spmd, body=%wide.region_23.24_spmd.sunk | while | flops 512869376 | bytes 71793240 | solution.py:346
  234.6 3.8 multiply_convert_fusion.6
  243.2 4.8 bitcast_add_fusion.11
  248.0 4.0 fusion.101
  252.0 3.4 reshape.517
  255.4 5.3 rev.15
  264.0 5.9 pad_maximum_fusion.1
  269.8 6.2 copy.115
  276.1 4.0 fusion.100
  280.1 3.4 reshape.515
  283.5 5.4 rev.14
  288.9 3.4 stack_reshape.6
  292.3 5.9 pad_maximum_fusion
  298.2 6.1 copy.114
  305.2 3.9 while.93
  305.4 3.7 fusion.223
  311.2 4.0 while.95
  311.4 3.7 fusion.230
  324.9 47.4 %reduce-scatter.9.cloned.1.call-done = f32[128,768]{1,0:T(8,128)} async-done(((f32[1024,768]{1,0:T(8,128)}), f32[128,768]{1,0:T(8,128)}) %reduce-scatter.9.cloned.1.call-update) | async-done | bytes 393232 | tf_op jit(solution)/shard_map/reduce_scatter | solution.py:356
  374.0 4.1 fusion.91
  379.0 29.9 %all_gather.49 = bf16[512,768]{1,0:T(8,128)(2,1)S(1)} all-gather(bf16[128,768]{1,0:T(8,128)(2,1)S(1)} %fusion.60), channel_id=1, replica_groups=mesh['ctx'=8,'fsdp'=4] {'fsdp'}, dimensions={0}, use_global_device_ids=true | all-gather | bytes 983040 | tf_op jit(solution)/shard_map/all_gather | solution.py:245
  408.9 5.4 multiply_convert_fusion.2
  417.3 29.8 %all-gather = bf16[1,512,768]{2,1,0:T(8,128)(2,1)S(1)} all-gather(bf16[1,128,768]{2,1,0:T(8,128)(2,1)} %param.31), channel_id=2, replica_groups=mesh['ctx'=8,'fsdp'=4] {'fsdp'}, dimensions={1}, use_global_device_ids=true | all-gather | bytes 983040 | tf_op jit(solution)/shard_map/all_gather | solution.py:246
  447.1 4.0 convert_reduce_fusion
  454.0 3.7 fusion.115
  460.0 112.0 %reduce-scatter.15.cloned.1.call-done = f32[192,2304]{1,0:T(8,128)} async-done(((f32[768,2304]{1,0:T(8,128)}), f32[192,2304]{1,0:T(8,128)}) %reduce-scatter.15.cloned.1.call-update) | async-done | bytes 1769488 | tf_op jit(solution)/shard_map/reduce_scatter | solution.py:372
  573.4 36.7 %reduce-scatter.7.cloned.1.call-done = f32[128,768]{1,0:T(8,128)} async-done(((f32[512,768]{1,0:T(8,128)}), f32[128,768]{1,0:T(8,128)}) %reduce-scatter.7.cloned.1.call-update) | async-done | bytes 393232 | tf_op jit(solution)/shard_map/reduce_scatter | solution.py:265
  612.5 34.6 %reduce-scatter.13.cloned.1.call-done = f32[128,768]{1,0:T(8,128)} async-done(((f32[512,768]{1,0:T(8,128)}), f32[128,768]{1,0:T(8,128)}) %reduce-scatter.13.cloned.1.call-update) | async-done | bytes 393232 | tf_op jit(solution)/shard_map/reduce_scatter | solution.py:266
  647.1 3.5 fusion.97
  652.2 17.1 %all-reduce.24 = (f32[768]{0:T(1024)S(1)}, f32[768]{0:T(1024)S(1)}, f32[768]{0:T(1024)S(1)}, f32[768]{0:T(1024)S(1)}, f32[2304]{0:T(1024)S(1)}, /*index=5*/f32[768]{0:T(1024)S(1)}) all-reduce(f32[768]{0:T(1024)S(1)} %get-tuple-element.643, f32[768]{0:T(1024)S(1)} %get-tuple-element.640, ...), channel_id=7, replica_groups=mesh['ctx'=8,'fsdp'=4] {'fsdp'}, use_global_device_ids=true, to_apply=%region_33.34.clone | all-reduce | flops 6144 | bytes 49152
  669.7 24.2 %all-reduce.22 = (f32[192]{0:T(256)}, f32[192]{0:T(256)}, f32[192]{0:T(256)}, f32[192]{0:T(256)}, f32[576]{0:T(1024)}, /*index=5*/f32[192]{0:T(256)S(1)}, f32[768]{0:T(1024)}) all-reduce(f32[192]{0:T(256)S(1)} %dynamic-slice.8, f32[192]{0:T(256)S(1)} %dynamic-slice.10, ...), channel_id=1, replica_groups=mesh['ctx'=8,'fsdp'=4] {'ctx'}, use_global_device_ids=true, to_apply=%region_34.35 | all-reduce | flops 2304 | bytes 18432 | tf_op jit(solution)/shard_map/psum | solution.py:377
  693.9 70.2 %all-reduce.28.cloned.1.call-done = (f32[192,2304]{1,0:T(8,128)}, f32[192,768]{1,0:T(8,128)}, f32[768,768]{1,0:T(8,128)}, f32[768,768]{1,0:T(8,128)}) async-done(((f32[192,2304]{1,0:T(8,128)}, f32[192,768]{1,0:T(8,128)}, f32[768,768]{1,0:T(8,128)}, f32[768,768]{1,0:T(8,128)}), (f32[192,2304]{1,0:T(8,128)}, f32[192,768]{1,0:T(8,128)}, f32[768,768]{1,0:T(8,128)}, ...) | async-done | bytes 7077904 | tf_op jit(solution)/shard_map/psum | solution.py:377
  (326 shorter events, 126.6 us)
Async XLA Ops:
  7.2 401.7 %copy-start = (bf16[768,768]{1,0:T(8,128)(2,1)S(1)}, bf16[768,768]{1,0:T(8,128)(2,1)}, u32[]{:S(2)}) copy-start(bf16[768,768]{1,0:T(8,128)(2,1)} %param.40) | copy-start | bytes 3538948
  7.2 33.6 %copy-start.18 = (bf16[1,128,768]{2,1,0:T(8,128)(2,1)S(1)}, bf16[1,128,768]{2,1,0:T(8,128)(2,1)}, u32[]{:S(2)}) copy-start(bf16[1,128,768]{2,1,0:T(8,128)(2,1)} %param.30) | copy-start | bytes 589828
  7.2 76.1 %all-gather.6.cloned.1.call-start = ((), (), s32[]{:S(2)}) async-start(), calls=%async_computation.6 | async-start | bytes 4423680 | tf_op jit(solution)/shard_map/all_gather | solution.py:133
  7.9 106.0 %all-gather.12.cloned.1.call-start = ((), (), s32[]{:S(2)}) async-start(), calls=%async_computation.9 | async-start | bytes 1474560 | tf_op jit(solution)/shard_map/all_gather | solution.py:135
  8.7 132.7 %all-gather.8.cloned.1.call-start = ((), (), s32[]{:S(2)}) async-start(), calls=%async_computation.7 | async-start | bytes 1769472 | tf_op jit(solution)/shard_map/all_gather | solution.py:170
  40.8 42.6 %copy-start.44 = (f32[768]{0:T(1024)}, f32[768]{0:T(1024)S(1)}, u32[]{:S(2)}) copy-start(f32[768]{0:T(1024)S(1)} %convert_element_type.96) | copy-start | bytes 9220
  40.8 42.6 %copy-start.50 = (f32[768]{0:T(1024)}, f32[768]{0:T(1024)S(1)}, u32[]{:S(2)}) copy-start(f32[768]{0:T(1024)S(1)} %convert_element_type.97) | copy-start | bytes 9220
  40.8 42.5 %copy-start.57 = (f32[128]{0:T(128)}, f32[128]{0:T(128)S(1)}, u32[]{:S(2)}) copy-start(f32[128]{0:T(128)S(1)} %broadcast_multiply_fusion.1) | copy-start | bytes 1540
  41.0 42.3 %copy-start.62 = (f32[128]{0:T(128)}, f32[128]{0:T(128)S(1)}, u32[]{:S(2)}) copy-start(f32[128]{0:T(128)S(1)} %fusion.63) | copy-start | bytes 1540
  41.1 42.3 %copy-start.59 = (f32[128]{0:T(128)}, f32[128]{0:T(128)S(1)}, u32[]{:S(2)}) copy-start(f32[128]{0:T(128)S(1)} %fusion.89) | copy-start | bytes 1540
  41.2 47.1 %copy-start.53 = (f32[128,8]{0,1:T(8,128)}, f32[128,8]{0,1:T(8,128)S(1)}, u32[]{:S(2)}) copy-start(f32[128,8]{0,1:T(8,128)S(1)} %get-tuple-element.854) | copy-start | bytes 12292
  41.2 47.1 %copy-start.55 = (f32[128,8]{0,1:T(8,128)}, f32[128,8]{0,1:T(8,128)S(1)}, u32[]{:S(2)}) copy-start(f32[128,8]{0,1:T(8,128)S(1)} %get-tuple-element.855) | copy-start | bytes 12292
  87.0 26.9 %copy-start.22 = (bf16[1,128,768]{2,1,0:T(8,128)(2,1)S(1)}, bf16[1,128,768]{2,1,0:T(8,128)(2,1)}, u32[]{:S(2)}) copy-start(bf16[1,128,768]{2,1,0:T(8,128)(2,1)} %param.31) | copy-start | bytes 589828
  89.9 79.6 %all-gather.10.cloned.1.call-start = ((), (), s32[]{:S(2)}) async-start(), calls=%async_computation.8 | async-start | bytes 1769472 | tf_op jit(solution)/shard_map/all_gather | solution.py:171
  120.5 201.9 %reduce-scatter.11.cloned.1.call-start = ((), (), s32[]{:S(2)}) async-start(), calls=%async_computation.12 | async-start | bytes 3538944 | tf_op jit(solution)/shard_map/reduce_scatter | solution.py:355
  214.6 17.2 %copy-start.10 = (bf16[64,12,64]{0,2,1:T(8,128)(2,1)S(1)}, bf16[64,12,64]{0,2,1:T(8,128)(2,1)}, u32[]{:S(2)}) copy-start(bf16[64,12,64]{0,2,1:T(8,128)(2,1)} %copy.113) | copy-start | bytes 294916
  217.6 3.9 copy-start.3
  221.5 2.7 copy-start.12
  234.6 3.8 copy-start.5
  238.5 2.7 copy-start.15
  276.1 96.3 %reduce-scatter.9.cloned.1.call-start = ((), (), s32[]{:S(2)}) async-start(), calls=%async_computation.11 | async-start | bytes 3538944 | tf_op jit(solution)/shard_map/reduce_scatter | solution.py:356
  304.4 155.6 %reduce-scatter.17.cloned.1.call-start = ((), (), s32[]{:S(2)}) async-start(), calls=%async_computation.15 | async-start | bytes 2949120 | tf_op jit(solution)/shard_map/reduce_scatter | solution.py:374
  305.2 6.0 copy-start.9
  305.2 6.0 copy-start.36
  305.2 6.0 copy-start.47
  311.2 5.3 copy-start.23
  318.5 253.5 %reduce-scatter.15.cloned.1.call-start = ((), (), s32[]{:S(2)}) async-start(), calls=%async_computation.14 | async-start | bytes 8847360 | tf_op jit(solution)/shard_map/reduce_scatter | solution.py:372
  320.0 3.7 copy-start.33
  320.0 3.7 copy-start.54
  320.0 3.7 copy-start.56
  324.7 49.3 %copy-start.19 = (bf16[1,128,768]{2,1,0:T(8,128)(2,1)S(1)}, bf16[1,128,768]{2,1,0:T(8,128)(2,1)}, u32[]{:S(2)}) copy-start(bf16[1,128,768]{2,1,0:T(8,128)(2,1)} %param.30) | copy-start | bytes 589828
  324.7 49.3 %copy-start.45 = (f32[768]{0:T(1024)S(1)}, f32[768]{0:T(1024)}, u32[]{:S(2)}) copy-start(f32[768]{0:T(1024)} %copy-done.44) | copy-start | bytes 9220
  324.7 49.3 %copy-start.51 = (f32[768]{0:T(1024)S(1)}, f32[768]{0:T(1024)}, u32[]{:S(2)}) copy-start(f32[768]{0:T(1024)} %copy-done.50) | copy-start | bytes 9220
  324.7 49.3 %copy-start.58 = (f32[128]{0:T(128)S(1)}, f32[128]{0:T(128)}, u32[]{:S(2)}) copy-start(f32[128]{0:T(128)} %copy-done.57) | copy-start | bytes 1540
  324.7 49.3 %copy-start.60 = (f32[128]{0:T(128)S(1)}, f32[128]{0:T(128)}, u32[]{:S(2)}) copy-start(f32[128]{0:T(128)} %copy-done.59) | copy-start | bytes 1540
  378.2 231.9 %reduce-scatter.7.cloned.1.call-start = ((), (), s32[]{:S(2)}) async-start(), calls=%async_computation.10 | async-start | bytes 1966080 | tf_op jit(solution)/shard_map/reduce_scatter | solution.py:265
  408.9 6.4 copy-start.70
  417.3 229.8 %reduce-scatter.13.cloned.1.call-start = ((), (), s32[]{:S(2)}) async-start(), calls=%async_computation.13 | async-start | bytes 1966080 | tf_op jit(solution)/shard_map/reduce_scatter | solution.py:266
  454.0 310.2 %all-reduce.28.cloned.1.call-start = ((), (), s32[]{:S(2)}) async-start(), calls=%async_computation.16 | async-start | bytes 14155776 | tf_op jit(solution)/shard_map/psum | solution.py:377
  454.0 3.7 copy-start.28
  612.5 38.1 %copy-start.63 = (f32[128]{0:T(128)S(1)}, f32[128]{0:T(128)}, u32[]{:S(2)}) copy-start(f32[128]{0:T(128)} %copy-done.62) | copy-start | bytes 1540
  612.5 38.6 %copy-start.24 = (bf16[1,128,768]{2,1,0:T(8,128)(2,1)S(1)}, bf16[1,128,768]{2,1,0:T(8,128)(2,1)}, u32[]{:S(2)}) copy-start(bf16[1,128,768]{2,1,0:T(8,128)(2,1)} %param.31) | copy-start | bytes 589828
  647.1 3.6 copy-start.20
  650.6 19.1 %copy-start.61 = (f32[768]{0:T(1024)S(1)}, f32[768]{0:T(1024)}, u32[]{:S(2)}) copy-start(f32[768]{0:T(1024)} %get-tuple-element.862) | copy-start | bytes 9220
  693.9 73.7 %copy-start.69 = (f32[192]{0:T(256)}, f32[192]{0:T(256)S(1)}, u32[]{:S(2)}) copy-start(f32[192]{0:T(256)S(1)} %get-tuple-element.1623) | copy-start | bytes 2308
  764.7 3.0 copy-start.41
  764.7 3.8 copy-start.26
  768.5 2.5 copy-start.25
  (35 other events, 46.7 us)
Sparse Core Ops, SparseCore 0:
  9.6 73.6 all-gather.5
  84.9 28.9 all-gather.11
  116.4 24.9 all-gather.7
  143.7 25.6 all-gather.9
  276.2 46.2 reduce-scatter.10
  326.1 46.2 reduce-scatter.8
  375.2 71.0 reduce-scatter.16
  448.6 123.2 reduce-scatter.14
  574.3 35.7 reduce-scatter.6
  612.8 34.2 reduce-scatter.12
  651.4 112.7 all-reduce.27
where the time goes:
time: 790 us; the launch traced here: 779 us
  waiting for transfers between devices  399 us (51%)
  local copies, waits for them, and re-layouts  130 us (16%)
  blocking collectives  123 us (16%)
  matrix products  81.5 us (10%)
  other arithmetic  25.9 us (3%)
  between operations  17.4 us (2%)
    reduce_scatter x1, waiting for transfers between devices, shards(): lax.psum_scatter(qkv_dweight, 'fsdp', scatter_dimension=0, tiled=True)  112 us
    psum x1, waiting for transfers between devices, shards(): lax.psum((shares[0], shares[1], shares[2], shares[3], shares[4], shares[5...  70.2 us
    reduce_scatter x1, waiting for transfers between devices, shards(): lax.psum_scatter(value_stored, 'ctx', scatter_dimension=0, tiled=True)  47.4 us
    all_gather x1, waiting for transfers between devices, shards(): lax.all_gather(qkv_weight, 'fsdp', axis=0, tiled=True)  42.2 us
    unnamed x2, blocking collectives  39.5 us
    reduce_scatter x1, waiting for transfers between devices, shards(): lax.psum_scatter(ffn_part, 'fsdp', scatter_dimension=0, tiled=True)  36.7 us
    reduce_scatter x1, waiting for transfers between devices, shards(): lax.psum_scatter(second_part, 'fsdp', scatter_dimension=0, tiled=True)  34.6 us
    all_gather x1, blocking collectives, shards(): lax.all_gather(second_in, 'fsdp', axis=0, tiled=True)  29.9 us
  transfers between devices with their start and end apart: 11, of which 10 were waited for; matrix products, arithmetic and copies ran while one was open for 15% of the time, Pallas kernels for 0%

commit v1 on v0

--- a/solution.py
+++ b/solution.py
@@ -3,7 +3,10 @@
 import jax
 import jax.numpy as jnp
 from jax import lax
+from jax.experimental import pallas as pl
+from jax.experimental.pallas import tpu as pltpu
 from jax.sharding import PartitionSpec as P
+import numpy as np
 
 HEADS = 12
 HEAD_DIM = 64
@@ -408,6 +411,686 @@
     )
 
 
+F32 = jnp.float32
+BF16 = jnp.bfloat16
+GROUPS = 4
+GROUP_HEADS = HEADS // GROUPS
+GROUP_COLS = GROUP_HEADS * HEAD_DIM
+EXTRA = 16
+
+
+def fits(mesh):
+    return mesh.shape["ctx"] == 2 * GROUPS and mesh.shape["fsdp"] == GROUPS
+
+
+def mm(left, right):
+    return jnp.dot(left, right, preferred_element_type=F32)
+
+
+def mm_nt(left, right):
+    return lax.dot_general(left, right, (((1,), (1,)), ((), ())), preferred_element_type=F32)
+
+
+def mm_tn(left, right):
+    return lax.dot_general(left, right, (((0,), (0,)), ((), ())), preferred_element_type=F32)
+
+
+def local_call(name, body, places, ins, outs, scratch=(), flops=0):
+    moved = sum(math.prod(i.shape) * i.dtype.itemsize for i in ins)
+    moved += sum(math.prod(s) * jnp.dtype(d).itemsize for s, d in outs)
+    return pl.pallas_call(
+        body,
+        out_shape=[jax.ShapeDtypeStruct(s, d) for s, d in outs],
+        in_specs=[pl.BlockSpec(memory_space=pltpu.SMEM)]
+        + [pl.BlockSpec(memory_space=pltpu.VMEM)] * len(ins),
+        out_specs=[pl.BlockSpec(memory_space=pltpu.VMEM)] * len(outs),
+        scratch_shapes=list(scratch),
+        compiler_params=pltpu.CompilerParams(vmem_limit_bytes=40 * 2**20),
+        cost_estimate=pl.CostEstimate(flops=flops, bytes_accessed=moved, transcendentals=0),
+        name=name,
+    )(places, *ins)
+
+
+def normed(values):
+    center = values - jnp.mean(values, axis=-1, keepdims=True)
+    spread = jnp.mean(center * center, axis=-1, keepdims=True)
+    scale = lax.rsqrt(spread + 1e-05)
+    return center * scale, scale
+
+
+def rotary_tables(rows, devices):
+    half = rows // 2
+    order = np.arange(rows * devices)
+    device, within = order // rows, order % rows
+    position = np.where(
+        within < half, device * half + within, (2 * devices - 1 - device) * half + within - half
+    )
+    pairs = ROT_DIMS // 2
+    inverse = np.power(10000.0, -2.0 * np.arange(pairs) / ROT_DIMS).astype(np.float32)
+    angle = (position.astype(np.float32)[:, None] * inverse[None, :]).astype(np.float32)
+    cosine = np.ones((rows * devices, HEAD_DIM), np.float32)
+    sine = np.zeros((rows * devices, HEAD_DIM), np.float32)
+    cosine[:, :pairs] = cosine[:, pairs:ROT_DIMS] = np.cos(angle)
+    sine[:, :pairs] = -np.sin(angle)
+    sine[:, pairs:ROT_DIMS] = np.sin(angle)
+    return np.tile(cosine, (1, 2)), np.tile(sine, (1, 2))
+
+
+def swapped(values):
+    lanes = values.shape[1]
+    place = lax.broadcasted_iota(jnp.int32, values.shape, 1) % HEAD_DIM
+    return jnp.where(
+        place < ROT_DIMS // 2,
+        pltpu.roll(values, lanes - ROT_DIMS // 2, 1),
+        pltpu.roll(values, ROT_DIMS // 2, 1),
+    )
+
+
+def vector_body(places, p0, p1, p2, p3, vec, bias, box):
+    z, group = places[1], places[0] // 2
+    rows = p0.shape[0] - EXTRA
+    shard = vec.shape[1] // GROUPS
+    for k, piece in enumerate((p0, p1, p2, p3)):
+        box[z ^ k] = piece[rows:, :].astype(F32)
+    units = []
+    for owner in range(GROUPS):
+        block = box[owner]
+        for item in range(6):
+            vec[item : item + 1, owner * shard : (owner + 1) * shard] = block[
+                item // 3 : item // 3 + 1, (item % 3) * shard : (item % 3 + 1) * shard
+            ]
+        for unit in range(3):
+            units.append(block[2:3, unit * GROUP_COLS : (unit + 1) * GROUP_COLS])
+    for slot, base in enumerate((GROUPS, 0, 2 * GROUPS)):
+        own = units[base]
+        for g in range(1, GROUPS):
+            own = jnp.where(group == g, units[base + g], own)
+        bias[0:1, slot * GROUP_COLS : (slot + 1) * GROUP_COLS] = own
+
+
+def qkv_body(places, *refs):
+    xs, gs, near, far = refs[0:4], refs[4:8], refs[8:12], refs[12:16]
+    vec, bias, out_near, out_far, cos_tab, sin_tab = refs[16:22]
+    fi, w, q_out, k_out, v_out, ag_out, ow, g_half, cos, sin = refs[22:]
+    c, z = places[0], places[1]
+    core = c % 2
+    width = w.shape[0]
+    shard = width // GROUPS
+    part = shard // 2
+    rows = xs[0].shape[0]
+    half = rows // 2
+    for k in range(GROUPS):
+        base = (z ^ k) * shard
+        w[pl.ds(pl.multiple_of(base + core * part, part), part), :] = near[k][0:part, :]
+        w[pl.ds(pl.multiple_of(base + (1 - core) * part, part), part), :] = far[k][0:part, :]
+    ow[pl.ds(pl.multiple_of(core * part, part), part), :] = out_near[...]
+    ow[pl.ds(pl.multiple_of((1 - core) * part, part), part), :] = out_far[...]
+    gain, shift = vec[0:1, :], vec[1:2, :]
+    two = 2 * GROUP_COLS
+    for side in range(2):
+        for j in range(GROUPS):
+            source = c ^ (2 * j)
+            to = slice((side * GROUPS + j) * half, (side * GROUPS + j + 1) * half)
+            at = pl.ds(pl.multiple_of(source * rows + side * half, half), half)
+            norm, _ = normed(xs[j][side * half : (side + 1) * half, :].astype(F32))
+            fi[to, :] = (norm * gain + shift).astype(BF16)
+            g_half[to, :] = gs[j][side * half : (side + 1) * half, :]
+            cos[to, :] = cos_tab[at, :]
+            sin[to, :] = sin_tab[at, :]
+    step = 2 * rows
+    for i in range(GROUPS * rows // step):
+        at = slice(i * step, (i + 1) * step)
+        chunk = fi[at, :]
+        kq = mm(chunk, w[:, :two]) + bias[0:1, :two]
+        c3 = jnp.concatenate([cos[at, :]] * 3, axis=1)
+        s3 = jnp.concatenate([sin[at, :]] * 3, axis=1)
+        kq = kq * c3 + swapped(kq) * s3
+        k_out[at, :] = kq[:, :GROUP_COLS].astype(BF16)
+        q_out[at, :] = (kq[:, GROUP_COLS:] * HEAD_DIM**-0.5).astype(BF16)
+        v_out[at, :] = (mm(chunk, w[:, two:]) + bias[0:1, two:]).astype(BF16)
+        ag_out[at, :] = mm_nt(g_half[at, :], ow[...]).astype(BF16)
+
+
+def attend_body(places, *refs):
+    q, k, v, k_far, v_far, ag, g_half, ow = refs[0:8]
+    batt = refs[8:12]
+    dw_keep, dw_send, dkq, dv_out, far_out = refs[12:17]
+    kbuf, vbuf, att, dwbuf = refs[17:]
+    c = places[0]
+    core = c % 2
+    rows = batt[0].shape[0]
+    half = rows // 2
+    low = GROUPS * half
+    devices = 2 * GROUPS
+    for side in range(2):
+        for part, (kr, vr) in enumerate(((k, v), (k_far, v_far))):
+            to = slice((2 * side + part) * low, (2 * side + part + 1) * low)
+            kbuf[to, :] = kr[side * low : (side + 1) * low, :]
+            vbuf[to, :] = vr[side * low : (side + 1) * low, :]
+
+    def token_pos(index, far):
+        device = (c ^ (2 * (index // half))) ^ far
+        return device * half + index % half
+
+    q_place = token_pos(lax.broadcasted_iota(jnp.int32, (low, 1), 0), 0)
+    k_index = lax.broadcasted_iota(jnp.int32, (1, 2 * low), 1)
+    k_place = token_pos(k_index % low, k_index // low)
+
+    def mirrored(place):
+        return (2 * devices - 1 - place // half) * half + place % half
+
+    allowed = (k_place <= q_place, mirrored(k_place) <= mirrored(q_place))
+
+    for head in range(GROUP_HEADS):
+        lanes = slice(head * HEAD_DIM, (head + 1) * HEAD_DIM)
+        lanes2 = slice(GROUP_COLS + head * HEAD_DIM, GROUP_COLS + (head + 1) * HEAD_DIM)
+        kh, vh = kbuf[:, lanes], vbuf[:, lanes]
+        dk_parts, dv_parts = [], []
+        for side in range(2):
+            at = slice(side * low, (side + 1) * low)
+            qh, gh = q[at, lanes], ag[at, lanes]
+            spans = [slice(0, 2 * low)] if side == 0 else [slice(0, 2 * low), slice(2 * low, 4 * low)]
+            scores = [mm_nt(qh, kh[s]) for s in spans]
+            scores[-1] = jnp.where(allowed[side], scores[-1], -1000000000.0)
+            top = jnp.max(scores[0], axis=-1, keepdims=True)
+            for s in scores[1:]:
+                top = jnp.maximum(top, jnp.max(s, axis=-1, keepdims=True))
+            raised = [jnp.exp(s - top) for s in scores]
+            total = sum(jnp.sum(r, axis=-1, keepdims=True) for r in raised)
+            inverse = 1.0 / total
+            probs = [r * inverse for r in raised]
+            low_probs = [p.astype(BF16) for p in probs]
+            mixed = sum(mm(p, vh[s]) for p, s in zip(low_probs, spans))
+            att[at, lanes] = mixed.astype(BF16)
+            prob_grads = [mm_nt(gh, vh[s]) for s in spans]
+            inner = sum(
+                jnp.sum(p * d, axis=-1, keepdims=True) for p, d in zip(probs, prob_grads)
+            )
+            score_grads = [(p * (d - inner)).astype(BF16) for p, d in zip(probs, prob_grads)]
+            dkq[at, lanes2] = sum(mm(s, kh[a]) for s, a in zip(score_grads, spans)) * HEAD_DIM**-0.5
+            dk_parts.append([mm_tn(s, qh) for s in score_grads])
+            dv_parts.append([mm_tn(p, gh) for p in low_probs])
+        dk = (dk_parts[0][0] + dk_parts[1][0], dk_parts[1][1])
+        dv = (dv_parts[0][0] + dv_parts[1][0], dv_parts[1][1])
+        for side in range(2):
+            at = slice(side * low, (side + 1) * low)
+            dkq[at, lanes] = dk[side][:low]
+            dv_out[at, lanes] = dv[side][:low]
+            far_out[at, lanes] = dk[side][low:].astype(BF16)
+            far_out[at, lanes2] = dv[side][low:].astype(BF16)
+    for side in range(2):
+        at = slice(side * low, (side + 1) * low)
+        branch = mm(att[at, :], ow[...])
+        for j in range(GROUPS):
+            batt[j][side * half : (side + 1) * half, :] = branch[
+                j * half : (j + 1) * half, :
+            ].astype(batt[j].dtype)
+    dwbuf[...] = mm_tn(att[...], g_half[...])
+    part = GROUP_COLS // 2
+    dw_keep[...] = dwbuf[pl.ds(pl.multiple_of(core * part, part), part), :]
+    dw_send[...] = dwbuf[pl.ds(pl.multiple_of((1 - core) * part, part), part), :].astype(BF16)
+
+
+def joined_body(places, *refs):
+    dkq, dv, far, w, fi, cos, sin, vec, ffn_vec = refs[0:9]
+    xs, g_own = refs[9:13], refs[13]
+    cas = refs[14:18]
+    keep, send = refs[18:20]
+    jgkq, jgv, dwbuf, first, ext = refs[20:]
+    c, z = places[0], places[1]
+    core, group = c % 2, c // 2
+    rows = g_own.shape[0]
+    half = rows // 2
+    width = w.shape[0]
+    shard = width // GROUPS
+    part = shard // 2
+    two = 2 * GROUP_COLS
+    step = 2 * rows
+    gain = vec[0:1, :]
+    bias_kq = jnp.zeros((1, two), F32)
+    bias_v = jnp.zeros((1, GROUP_COLS), F32)
+    for i in range(GROUPS * rows // step):
+        at = slice(i * step, (i + 1) * step)
+        other = far[at, :].astype(F32)
+        dk = dkq[at, :GROUP_COLS] + other[:, :GROUP_COLS]
+        kq = jnp.concatenate([dk, dkq[at, GROUP_COLS:]], axis=1)
+        c3 = jnp.concatenate([cos[at, :]] * 3, axis=1)
+        s3 = jnp.concatenate([sin[at, :]] * 3, axis=1)
+        low_kq = (kq * c3 - swapped(kq) * s3).astype(BF16)
+        low_v = (dv[at, :] + other[:, GROUP_COLS:]).astype(BF16)
+        jgkq[at, :] = low_kq
+        jgv[at, :] = low_v
+        bias_kq += jnp.sum(low_kq.astype(F32), axis=0, keepdims=True)
+        bias_v += jnp.sum(low_v.astype(F32), axis=0, keepdims=True)
+        first[at, :] = mm_nt(low_kq, w[:, :two]) + mm_nt(low_v, w[:, two:])
+    dgain = jnp.zeros((1, width), F32)
+    dshift = jnp.zeros((1, width), F32)
+    for side in range(2):
+        for j in range(GROUPS):
+            at = slice((side * GROUPS + j) * half, (side * GROUPS + j + 1) * half)
+            mine = slice(side * half, (side + 1) * half)
+            norm, _ = normed(xs[j][mine, :].astype(F32))
+            grad = first[at, :]
+            dgain += jnp.sum(grad * norm, axis=0, keepdims=True)
+            dshift += jnp.sum(grad, axis=0, keepdims=True)
+            cas[j][mine, :] = (grad * gain).astype(cas[j].dtype)
+    gsum = jnp.sum(g_own[...].astype(F32), axis=0, keepdims=True)
+    dwbuf[:, :two] = mm_tn(fi[...], jgkq[...])
+    dwbuf[:, two:] = mm_tn(fi[...], jgv[...])
+    ext[...] = jnp.zeros_like(ext)
+    for owner in range(GROUPS):
+        own = slice(owner * shard, (owner + 1) * shard)
+        for slot in range(3):
+            unit = owner * 3 + slot
+            kind = unit // GROUPS
+            vector = (bias_kq[:, GROUP_COLS:], bias_kq[:, :GROUP_COLS], bias_v)[kind]
+            to = slice(slot * GROUP_COLS, (slot + 1) * GROUP_COLS)
+            ext[owner, 0:1, to] = jnp.where(group == unit % GROUPS, vector, 0.0)
+        here = z == owner
+        for slot, vector in enumerate((dgain[:, own], dshift[:, own], gsum[:, own])):
+            ext[owner, 1:2, slot * shard : (slot + 1) * shard] = vector
+        ext[owner, 2:3, 0:shard] = ffn_vec[0:1, own]
+        ext[owner, 2:3, shard : 2 * shard] = ffn_vec[1:2, own]
+        ext[owner, 2:3, 2 * shard : 3 * shard] = jnp.where(here, ffn_vec[2:3, 0:shard], 0.0)
+        ext[owner, 3:4, :] = jnp.where(here, ffn_vec[2:3, shard:], 0.0)
+    for k in range(GROUPS):
+        owner = z ^ k
+        base = owner * shard
+        keep[k, 0:part, :] = dwbuf[pl.ds(pl.multiple_of(base + core * part, part), part), :]
+        send[k, 0:part, :] = dwbuf[
+            pl.ds(pl.multiple_of(base + (1 - core) * part, part), part), :
+        ].astype(BF16)
+        keep[k, part:, :] = ext[owner].astype(BF16).astype(F32)
+        send[k, part:, :] = ext[owner].astype(BF16)
+
+
+def split_sum_body(places, keep, got, own, *sends):
+    for k in range(GROUPS):
+        total = keep[k] + got[k].astype(F32)
+        if k == 0:
+            own[...] = total
+        else:
+            sends[k - 1][...] = total.astype(BF16)
+
+
+def sum_body(places, own, a, b, c, out):
+    out[...] = (own[...] + a[...].astype(F32) + b[...].astype(F32) + c[...].astype(F32)).astype(
+        out.dtype
+    )
+
+
+def ffn_body(places, *refs):
+    xs, gs = refs[0:4], refs[4:8]
+    up_w, down_w, up_b, vec = refs[8:12]
+    parts, cas = refs[12:16], refs[16:20]
+    keep, send, sums = refs[20:23]
+    si, gb, active, hidden_grad, second, dwbuf = refs[23:]
+    c, z = places[0], places[1]
+    rows = xs[0].shape[0]
+    width = up_w.shape[0]
+    hid = up_w.shape[1]
+    gain, shift = vec[2:3, :], vec[3:4, :]
+    for k in range(GROUPS):
+        at = slice(k * rows, (k + 1) * rows)
+        norm, _ = normed(xs[k][...].astype(F32))
+        si[at, :] = (norm * gain + shift).astype(BF16)
+        gb[at, :] = gs[k][...]
+    step = 2 * rows
+    bias_sum = jnp.zeros((1, hid), F32)
+    for i in range(GROUPS * rows // step):
+        at = slice(i * step, (i + 1) * step)
+        hidden = mm(si[at, :], up_w[...]) + up_b[...].astype(F32)
+        cdf = 0.5 + 0.5 * lax.erf(hidden * (0.5**0.5))
+        density = jnp.exp(hidden * hidden * -0.5) * (1.0 / math.sqrt(2.0 * math.pi))
+        active[at, :] = (hidden * cdf).astype(BF16)
+        grad = (mm_nt(gb[at, :], down_w[...]) * (cdf + hidden * density)).astype(BF16)
+        hidden_grad[at, :] = grad
+        bias_sum += jnp.sum(grad.astype(F32), axis=0, keepdims=True)
+        part = mm(active[at, :], down_w[...])
+        second[at, :] = mm_nt(grad, up_w[...])
+        for k in range(2):
+            piece = parts[2 * i + k]
+            piece[...] = part[k * rows : (k + 1) * rows, :].astype(piece.dtype)
+    dgain = jnp.zeros((1, width), F32)
+    dshift = jnp.zeros((1, width), F32)
+    for k in range(GROUPS):
+        at = slice(k * rows, (k + 1) * rows)
+        norm, _ = normed(xs[k][...].astype(F32))
+        grad = second[at, :]
+        dgain += jnp.sum(grad * norm, axis=0, keepdims=True)
+        dshift += jnp.sum(grad, axis=0, keepdims=True)
+        cas[k][...] = (grad * gain).astype(cas[k].dtype)
+    sums[0:1, :] = dgain
+    sums[1:2, :] = dshift
+    sums[2:3, :] = bias_sum
+    dwbuf[0:width, :] = mm_tn(si[...], hidden_grad[...])
+    dwbuf[width:, :] = mm_tn(active[...], gb[...])
+    chunk = (width + hid) // (2 * GROUPS)
+    for j in range(GROUPS):
+        near = c ^ (2 * j)
+        keep[j] = dwbuf[pl.ds(pl.multiple_of(near * chunk, chunk), chunk), :]
+        far = near ^ 1
+        send[j] = dwbuf[pl.ds(pl.multiple_of(far * chunk, chunk), chunk), :].astype(BF16)
+
+
+def spread_body(places, *refs):
+    near, far = refs[0:4], refs[4:8]
+    up_dw, down_dw, buf = refs[8:]
+    c = places[0]
+    chunk = near[0].shape[0]
+    for j in range(GROUPS):
+        place = c ^ (2 * j)
+        buf[pl.ds(pl.multiple_of(place * chunk, chunk), chunk), :] = near[j][...].astype(F32)
+        buf[pl.ds(pl.multiple_of((place ^ 1) * chunk, chunk), chunk), :] = far[j][...].astype(F32)
+    up_dw[...] = buf[0 : up_dw.shape[0], :]
+    down_dw[...] = buf[up_dw.shape[0] :, :]
+
+
+def finish_body(places, *refs):
+    near, far = refs[0:4], refs[4:8]
+    qkv_dw, vec, bias, up_db, box, tail = refs[8:]
+    c = places[0]
+    core, group = c % 2, c // 2
+    part = near[0].shape[0] - EXTRA
+    shard = 2 * part
+    for j in range(GROUPS):
+        place = group ^ j
+        tail[place] = near[j][part:, :].astype(F32)
+        box[place, pl.ds(pl.multiple_of(core * part, part), part), :] = near[j][0:part, :].astype(F32)
+        box[place, pl.ds(pl.multiple_of((1 - core) * part, part), part), :] = far[j][
+            0:part, :
+        ].astype(F32)
+    for g in range(GROUPS):
+        for kind, slot in enumerate((1, 0, 2)):
+            at = (kind * GROUPS + g) * GROUP_COLS
+            qkv_dw[:, at : at + GROUP_COLS] = box[
+                g, :, slot * GROUP_COLS : (slot + 1) * GROUP_COLS
+            ]
+    total = tail[0] + tail[1] + tail[2] + tail[3]
+    bias[...] = total[0:1, :]
+    for slot in range(3):
+        vec[slot : slot + 1, :] = total[1:2, slot * shard : (slot + 1) * shard]
+    vec[3:4, :] = total[2:3, 0:shard]
+    vec[4:5, :] = total[2:3, shard : 2 * shard]
+    up_db[0:1, 0:shard] = total[2:3, 2 * shard :]
+    up_db[0:1, shard:] = total[3:4, :]
+
+
+def token_body(places, *refs):
+    x, g, vec = refs[0:3]
+    outs, grads = refs[3:11], refs[11:19]
+    layer_out, input_grad = refs[19:]
+    values = x[...].astype(F32)
+    total = values + vec[4:5, :] + vec[5:6, :]
+    for piece in outs:
+        total += piece[...].astype(F32)
+    layer_out[...] = total.astype(BF16)
+    norm, scale = normed(values)
+    cot = grads[0][...]
+    for piece in grads[1:]:
+        cot += piece[...].astype(F32)
+    shifted = cot - jnp.mean(cot, axis=-1, keepdims=True)
+    shifted -= norm * jnp.mean(cot * norm, axis=-1, keepdims=True)
+    input_grad[...] = g[...].astype(F32) + scale * shifted
+
+
+def block_shards(
+    tokens,
+    cotangent,
+    att_gain,
+    att_shift,
+    ffn_gain,
+    ffn_shift,
+    qkv_weight,
+    qkv_bias,
+    out_weight,
+    out_bias,
+    up_weight,
+    up_bias,
+    down_weight,
+    down_bias,
+):
+    width = tokens.shape[-1]
+    x = tokens.reshape(-1, width)
+    g = cotangent.reshape(-1, width)
+    rows = x.shape[0]
+    n_ctx, n_z = lax.axis_size("ctx"), lax.axis_size("fsdp")
+    c, z = lax.axis_index("ctx"), lax.axis_index("fsdp")
+    core, group = c % 2, c // 2
+    shard = width // n_z
+    part = shard // 2
+    hid = up_weight.shape[1]
+    places = jnp.stack([c, z]).astype(jnp.int32)
+    three = 3 * GROUP_COLS
+    near_rows = GROUPS * rows
+
+    def over_ctx(value, k):
+        return lax.ppermute(value, "ctx", [(i, i ^ k) for i in range(n_ctx)])
+
+    def over_z(value, k):
+        return lax.ppermute(value, "fsdp", [(i, i ^ k) for i in range(n_z)])
+
+    def over_both(value, pairs):
+        return lax.ppermute(
+            value, ("ctx", "fsdp"), [(a * n_z + b, d * n_z + e) for a, b, d, e in pairs]
+        )
+
+    def chips(value):
+        return [value] + [over_ctx(value, 2 * j) for j in range(1, GROUPS)]
+
+    vectors = jnp.concatenate(
+        [att_gain, att_shift, ffn_gain, ffn_shift, out_bias, down_bias, qkv_bias]
+    ).reshape(3, three)
+    columns = [
+        lax.dynamic_slice(qkv_weight, (core * part, base * width + group * GROUP_COLS), (part, GROUP_COLS))
+        for base in (1, 0, 2)
+    ]
+    payload = jnp.concatenate(
+        [jnp.concatenate(columns, axis=1), jnp.pad(vectors, ((0, EXTRA - 3), (0, 0)))], axis=0
+    )
+    near_w = [payload] + [over_z(payload, k) for k in range(1, n_z)]
+    far_w = [over_ctx(p, 1) for p in near_w]
+    own_out = lax.dynamic_slice(out_weight, (core * part, 0), (part, width))
+    got = [
+        over_both(own_out, [(a, a // 2, a, (a // 2) ^ k) for a in range(n_ctx)]) for k in range(1, n_z)
+    ]
+    out_near = jnp.where(z == group, own_out, got[0] + got[1] + got[2])
+    out_far = over_ctx(out_near, 1)
+
+    x_plane, g_plane = chips(x), chips(g)
+    x_line = [x] + [over_z(x, k) for k in range(1, n_z)]
+    g_line = [g] + [over_z(g, k) for k in range(1, n_z)]
+
+    vec, bias = local_call(
+        "vectors",
+        vector_body,
+        places,
+        near_w,
+        [((8, width), F32), ((8, three), F32)],
+        [pltpu.VMEM((GROUPS, EXTRA, three), F32)],
+    )
+    cos_tab, sin_tab = rotary_tables(rows, n_ctx)
+    fi, w, q, k, v, ag, ow, g_half, cos, sin = local_call(
+        "qkv",
+        qkv_body,
+        places,
+        [*x_plane, *g_plane, *near_w, *far_w, vec, bias, out_near, out_far, cos_tab, sin_tab],
+        [
+            ((near_rows, width), BF16),
+            ((width, three), BF16),
+            ((near_rows, GROUP_COLS), BF16),
+            ((near_rows, GROUP_COLS), BF16),
+            ((near_rows, GROUP_COLS), BF16),
+            ((near_rows, GROUP_COLS), BF16),
+            ((GROUP_COLS, width), BF16),
+            ((near_rows, width), BF16),
+            ((near_rows, 128), F32),
+            ((near_rows, 128), F32),
+        ],
+        flops=2 * near_rows * width * 4 * GROUP_COLS,
+    )
+    k_far, v_far = over_ctx(k, 1), over_ctx(v, 1)
+    att_outs = local_call(
+        "attend",
+        attend_body,
+        places,
+        [q, k, v, k_far, v_far, ag, g_half, ow],
+        [((rows, width), F32)]
+        + [((rows, width), BF16)] * 3
+        + [
+            ((part, width), F32),
+            ((part, width), BF16),
+            ((near_rows, 2 * GROUP_COLS), F32),
+            ((near_rows, GROUP_COLS), F32),
+            ((near_rows, 2 * GROUP_COLS), BF16),
+        ],
+        [
+            pltpu.VMEM((2 * near_rows, GROUP_COLS), BF16),
+            pltpu.VMEM((2 * near_rows, GROUP_COLS), BF16),
+            pltpu.VMEM((near_rows, GROUP_COLS), BF16),
+            pltpu.VMEM((GROUP_COLS, width), F32),
+        ],
+        flops=2 * 7 * 256 * GROUP_HEADS * near_rows * 2 * near_rows,
+    )
+    batt, (dw_keep, dw_send, dkq, dv, far_dkv) = att_outs[:4], att_outs[4:]
+    far_dkv = over_ctx(far_dkv, 1)
+    branch_att = [batt[0]] + [over_ctx(batt[j], 2 * j) for j in range(1, GROUPS)]
+
+    ffn_outs = local_call(
+        "ffn",
+        ffn_body,
+        places,
+        [*x_line, *g_line, up_weight, down_weight, up_bias.reshape(1, -1), vec],
+        ([((rows, width), F32)] + [((rows, width), BF16)] * 3) * 2
+        + [
+            ((GROUPS, (width + hid) // n_ctx, width), F32),
+            ((GROUPS, (width + hid) // n_ctx, width), BF16),
+            ((8, width), F32),
+        ],
+        [
+            pltpu.VMEM((near_rows, width), BF16),
+            pltpu.VMEM((near_rows, width), BF16),
+            pltpu.VMEM((near_rows, hid), BF16),
+            pltpu.VMEM((near_rows, hid), BF16),
+            pltpu.VMEM((near_rows, width), F32),
+            pltpu.VMEM((width + hid, width), F32),
+        ],
+        flops=2 * 6 * near_rows * width * hid,
+    )
+    ffn_out, ffn_ca, (ffn_keep, ffn_send, ffn_sums) = ffn_outs[:4], ffn_outs[4:8], ffn_outs[8:]
+    branch_ffn = [ffn_out[0]] + [over_z(ffn_out[k], k) for k in range(1, n_z)]
+    second = [ffn_ca[0]] + [over_z(ffn_ca[k], k) for k in range(1, n_z)]
+
+    chunk = (width + hid) // n_ctx
+    own, *sends = local_call(
+        "ffn_pair",
+        split_sum_body,
+        places,
+        [ffn_keep, over_ctx(ffn_send, 1)],
+        [((chunk, width), F32)] + [((chunk, width), BF16)] * 3,
+    )
+    (total,) = local_call(
+        "ffn_sum",
+        sum_body,
+        places,
+        [own] + [over_ctx(sends[j - 1], 2 * j) for j in range(1, GROUPS)],
+        [((chunk, width), BF16)],
+    )
+    near = chips(total)
+    up_dw, down_dw = local_call(
+        "ffn_spread",
+        spread_body,
+        places,
+        near + [over_ctx(p, 1) for p in near],
+        [((width, hid), F32), ((hid, width), F32)],
+        [pltpu.VMEM((width + hid, width), F32)],
+    )
+
+    joined_outs = local_call(
+        "joined",
+        joined_body,
+        places,
+        [dkq, dv, far_dkv, w, fi, cos, sin, vec, ffn_sums, *x_plane, g],
+        [((rows, width), F32)]
+        + [((rows, width), BF16)] * 3
+        + [((n_z, part + EXTRA, three), F32), ((n_z, part + EXTRA, three), BF16)],
+        [
+            pltpu.VMEM((near_rows, 2 * GROUP_COLS), BF16),
+            pltpu.VMEM((near_rows, GROUP_COLS), BF16),
+            pltpu.VMEM((width, three), F32),
+            pltpu.VMEM((near_rows, width), F32),
+            pltpu.VMEM((GROUPS, EXTRA, three), F32),
+        ],
+        flops=2 * 2 * near_rows * width * three,
+    )
+    ca, (keep, send) = joined_outs[:4], joined_outs[4:]
+    first = [ca[0]] + [over_ctx(ca[j], 2 * j) for j in range(1, GROUPS)]
+    own, *sends = local_call(
+        "qkv_pair",
+        split_sum_body,
+        places,
+        [keep, over_ctx(send, 1)],
+        [((part + EXTRA, three), F32)] + [((part + EXTRA, three), BF16)] * 3,
+    )
+    (total,) = local_call(
+        "qkv_sum",
+        sum_body,
+        places,
+        [own] + [over_z(sends[k - 1], k) for k in range(1, n_z)],
+        [((part + EXTRA, three), BF16)],
+    )
+    near = chips(total)
+    qkv_dw, sums, qkv_db, up_db = local_call(
+        "qkv_finish",
+        finish_body,
+        places,
+        near + [over_ctx(p, 1) for p in near],
+        [((shard, 3 * width), F32), ((8, shard), F32), ((1, three), F32), ((1, hid), F32)],
+        [pltpu.VMEM((GROUPS, shard, three), F32), pltpu.VMEM((GROUPS, EXTRA, three), F32)],
+    )
+
+    mine = (dw_keep + over_ctx(dw_send, 1).astype(F32)).astype(BF16)
+    got = [
+        over_both(mine, [(a, (a // 2) ^ k, a, a // 2) for a in range(n_ctx)]) for k in range(1, n_z)
+    ]
+    mine = sum((p.astype(F32) for p in got), mine.astype(F32)).astype(BF16)
+    got = [
+        over_both(mine, [(a, a // 2, a ^ (2 * j), a // 2) for a in range(n_ctx)])
+        for j in range(1, GROUPS)
+    ]
+    out_near = jnp.where(z == group, mine, got[0] + got[1] + got[2])
+    out_far = over_ctx(out_near, 1)
+    out_dw = jnp.where(
+        core == 0,
+        jnp.concatenate([out_near, out_far], axis=0),
+        jnp.concatenate([out_far, out_near], axis=0),
+    ).astype(F32)
+
+    layer_out, input_grad = local_call(
+        "token",
+        token_body,
+        places,
+        [x, g, vec, *branch_att, *branch_ffn, *first, *second],
+        [((rows, width), BF16), ((rows, width), F32)],
+    )
+    return (
+        layer_out.reshape(tokens.shape),
+        input_grad.reshape(tokens.shape),
+        sums[0],
+        sums[1],
+        sums[3],
+        sums[4],
+        qkv_dw,
+        qkv_db[0],
+        out_dw,
+        sums[2],
+        up_dw,
+        up_db[0],
+        down_dw,
+        sums[2],
+    )
+
+
 def solution(mesh):
     in_specs = (
         P("fsdp", "ctx", None),
@@ -441,4 +1124,5 @@
         P("fsdp", None),
         P("fsdp"),
     )
-    return jax.shard_map(shards, mesh=mesh, in_specs=in_specs, out_specs=out_specs, check_vma=False)
+    per_device = block_shards if fits(mesh) else shards
+    return jax.shard_map(per_device, mesh=mesh, in_specs=in_specs, out_specs=out_specs, check_vma=False)

time: 790 us -> 235 us (0.30); the launches traced: 779 us -> 232 us
  waiting for transfers between devices: 399 us -> 90.3 us
  blocking collectives: 123 us -> 0 us
  local copies, waits for them, and re-layouts: 130 us -> 21.8 us
  starting transfers between devices: 0.45 us -> 85.7 us
  matrix products: 81.5 us -> 0 us
  Pallas kernels: 0 us -> 30 us
  other arithmetic: 25.9 us -> 3.37 us
  between operations: 17.4 us -> 1.26 us
    reduce_scatter x6 -> x0, waiting for transfers between devices: 233 us -> none  [the longest x1 112 us: shards(): lax.psum_scatter(qkv_dweight, 'fsdp', scatter_dimension=0, tiled=True)]
    all_gather x4 -> x0, waiting for transfers between devices: 94.4 us -> none  [the longest x1 42.2 us: shards(): lax.all_gather(qkv_weight, 'fsdp', axis=0, tiled=True)]
    ppermute x0 -> x68, waiting for transfers between devices: none -> 90.3 us  [the longest x18 49.2 us: over_z(): return lax.ppermute(value, 'fsdp', [(i, i ^ k) for i in range(n_z)])]
    ppermute x0 -> x68, starting transfers between devices: none -> 85.7 us  [the longest x18 35.7 us: over_z(): return lax.ppermute(value, 'fsdp', [(i, i ^ k) for i in range(n_z)])]
    dot_general x30 -> x0, matrix products: 81.5 us -> none  [the longest x6 10.5 us: scores_block(): jnp.einsum('qhd,khd->hqk', query_heads, key_heads, preferred_element_type...]
    psum x1 -> x0, waiting for transfers between devices: 70.2 us -> none  [shards(): lax.psum((shares[0], shares[1], shares[2], shares[3], shares[4], shares[5...]
    all_gather x2 -> x0, blocking collectives: 59.7 us -> none  [the longest x1 29.9 us: shards(): lax.all_gather(second_in, 'fsdp', axis=0, tiled=True)]
    unnamed x2 -> x0, blocking collectives: 39.5 us -> none
  transfers between devices with their start and end apart: 11 -> 68, of which waited for: 10 -> 19; matrix products, arithmetic and copies ran while one was open for 15% -> 2% of each run, Pallas kernels for 0% -> 12%
where the time goes in v1:
time: 235 us; the launch traced here: 232 us
  waiting for transfers between devices  90.3 us (38%)
  starting transfers between devices  85.7 us (36%)
  Pallas kernels  30 us (13%)
  local copies, waits for them, and re-layouts  21.8 us (9%)
  other arithmetic  3.37 us (1%)
    ppermute x18, waiting for transfers between devices, over_z(): return lax.ppermute(value, 'fsdp', [(i, i ^ k) for i in range(n_z)])  49.2 us
    ppermute x41, waiting for transfers between devices, over_ctx(): return lax.ppermute(value, 'ctx', [(i, i ^ k) for i in range(n_ctx)])  37.5 us
    ppermute x18, starting transfers between devices, over_z(): return lax.ppermute(value, 'fsdp', [(i, i ^ k) for i in range(n_z)])  35.7 us
    ppermute x41, starting transfers between devices, over_ctx(): return lax.ppermute(value, 'ctx', [(i, i ^ k) for i in range(n_ctx)])  31.7 us
    pallas_call x12, Pallas kernels, local_call(): pl.pallas_call(body, out_shape=[jax.ShapeDtypeStruct(s, d) for s, d in ou...  30 us
    ppermute x9, starting transfers between devices, over_both(): lax.ppermute(value, ('ctx', 'fsdp'), [(a * n_z + b, d * n_z + e) for a, b...  18.3 us
    unnamed x81, local copies, waits for them, and re-layouts  14.2 us
    concatenate x1, local copies, waits for them, and re-layouts, block_shards(): jnp.concatenate([att_gain, att_shift, ffn_gain, ffn_shift, out_bias, down...  4.9 us
  transfers between devices with their start and end apart: 68, of which 19 were waited for; matrix products, arithmetic and copies ran while one was open for 2% of the time, Pallas kernels for 12%

profile of v1, /device:TPU:0, one launch (start us, length us, event | category | flops | bytes accessed | tf_op | source)
XLA Modules:
  0.0 232.4 jit_solution(12547975824558804558)
XLA Ops:
  0.7 4.9 %concatenate.16 = bf16[1728]{0:T(1024)(128)(2,1)S(1)} concatenate(bf16[192]{0:T(256)(128)(2,1)} %param.18, bf16[192]{0:T(256)(128)(2,1)} %param.19, bf16[192]{0:T(256)(128)(2,1)} %param.20, bf16[192]{0:T(256)(128)(2,1)} %param.21, bf16[192]{0:T(256)(128)(2,1)} %param.25, bf16[192]{0:T(256)(128)(2,1)} %param.29, bf16[576]{0:T(1024)(128)(2,1)} %param.23), dimensions={0} | concatenate | bytes 6912 | tf_op jit(solution)/shard_map/concatenate | solution.py:881
  6.9 3.1 %collective-permute-start = (bf16[112,576]{1,0:T(8,128)(2,1)S(1)}, bf16[112,576]{1,0:T(8,128)(2,1)S(1)}, u32[]{:S(2)}, u32[]{:S(2)}) collective-permute-start(bf16[112,576]{1,0:T(8,128)(2,1)S(1)} %fusion.2.p0.refs_8_), channel_id=1, source_target_pairs={{0,1},{1,0},{2,3},{3,2},{4,5},{5,4},{6,7},{7,6},{8,9},{9,8},{10,11... | collective-permute-start | bytes 387080 | tf_op jit(solution)/shard_map/ppermute | solution.py:871
  10.0 2.6 %collective-permute-start.1 = (bf16[112,576]{1,0:T(8,128)(2,1)S(1)}, bf16[112,576]{1,0:T(8,128)(2,1)S(1)}, u32[]{:S(2)}, u32[]{:S(2)}) collective-permute-start(bf16[112,576]{1,0:T(8,128)(2,1)S(1)} %fusion.2.p0.refs_8_), channel_id=1, source_target_pairs={{0,2},{1,3},{2,0},{3,1},{4,6},{5,7},{6,4},{7,5},{8,10},{9,11},{10,... | collective-permute-start | bytes 387080 | tf_op jit(solution)/shard_map/ppermute | solution.py:871
  12.6 1.7 collective-permute-start.3
  15.2 5.5 %collective-permute-start.15 = (bf16[96,768]{1,0:T(8,128)(2,1)S(1)}, bf16[96,768]{1,0:T(8,128)(2,1)S(1)}, u32[]{:S(2)}, u32[]{:S(2)}) collective-permute-start(bf16[96,768]{1,0:T(8,128)(2,1)S(1)} %constant_dynamic-slice_fusion), channel_id=1, source_target_pairs={{0,3},{4,7},{9,10},{13,14},{18,17},{22,21},{27,24},{31,28}} | collective-permute-start | bytes 442376 | tf_op jit(solution)/shard_map/ppermute | solution.py:874
  22.0 1.7 collective-permute-done.1.p2.refs_10_
  23.7 1.4 collective-permute-start.14
  26.6 1.4 collective-permute-start.4
  28.0 3.5 %collective-permute-start.5 = (bf16[128,768]{1,0:T(8,128)(2,1)}, bf16[128,768]{1,0:T(8,128)(2,1)S(1)}, u32[]{:S(2)}, u32[]{:S(2)}) collective-permute-start(bf16[128,768]{1,0:T(8,128)(2,1)} %bitcast.13), channel_id=1, source_target_pairs={{0,24},{4,28},{8,16},{12,20},{16,8},{20,12},{24,0},{28,4},{1,25},{... | collective-permute-start | bytes 589832 | tf_op jit(solution)/shard_map/ppermute | solution.py:868
  32.1 1.5 collective-permute-start.7
  33.5 1.5 collective-permute-start.8
  36.0 2.8 %collective-permute-done.4.refs_2_.refs_11_ = bf16[128,768]{1,0:T(8,128)(2,1)S(1)} collective-permute-done((bf16[128,768]{1,0:T(8,128)(2,1)}, bf16[128,768]{1,0:T(8,128)(2,1)S(1)}, u32[]{:S(2)}, u32[]{:S(2)}) %collective-permute-start.4) | collective-permute-done | bytes 196640 | tf_op jit(solution)/shard_map/ppermute | solution.py:868
  39.3 2.9 %collective-permute-done.6.refs_5_ = bf16[128,768]{1,0:T(8,128)(2,1)S(1)} collective-permute-done((bf16[128,768]{1,0:T(8,128)(2,1)}, bf16[128,768]{1,0:T(8,128)(2,1)S(1)}, u32[]{:S(2)}, u32[]{:S(2)}) %collective-permute-start.6) | collective-permute-done | bytes 196640 | tf_op jit(solution)/shard_map/ppermute | solution.py:868
  42.2 4.2 %collective-permute-done.7.refs_6_ = bf16[128,768]{1,0:T(8,128)(2,1)S(1)} collective-permute-done((bf16[128,768]{1,0:T(8,128)(2,1)}, bf16[128,768]{1,0:T(8,128)(2,1)S(1)}, u32[]{:S(2)}, u32[]{:S(2)}) %collective-permute-start.7) | collective-permute-done | bytes 196640 | tf_op jit(solution)/shard_map/ppermute | solution.py:868
  47.3 6.2 %collective-permute-start.22 = (bf16[128,768]{1,0:T(8,128)(2,1)S(1)}, bf16[128,768]{1,0:T(8,128)(2,1)S(1)}, u32[]{:S(2)}, u32[]{:S(2)}) collective-permute-start(bf16[128,768]{1,0:T(8,128)(2,1)S(1)} %bitcast.14), channel_id=1, source_target_pairs={{0,1},{1,0},{2,3},{3,2},{4,5},{5,4},{6,7},{7,6},{8,9},{9,8},{10,11... | collective-permute-start | bytes 589832 | tf_op jit(solution)/shard_map/ppermute | solution.py:871
  53.5 2.2 qkv.1
  56.2 2.3 collective-permute-start.23
  60.8 2.3 collective-permute-start.26
  63.1 1.5 collective-permute-start.27
  64.6 8.0 %attend.1 = (f32[128,768]{1,0:T(8,128)S(1)}, bf16[128,768]{1,0:T(8,128)(2,1)S(1)}, bf16[128,768]{1,0:T(8,128)(2,1)S(1)}, bf16[128,768]{1,0:T(8,128)(2,1)S(1)}, f...) custom-call(s32[2]{0:T(128)S(1)} %pad_add_fusion.places, ...), custom_call_target="tpu_custom_call" | custom-call | flops 5637144576 | bytes 5259264 | tf_op jit(solution)/shard_map/attend/pallas_call | solution.py:441
  73.4 16.8 %collective-permute-done.26.refs_6_ = bf16[128,768]{1,0:T(8,128)(2,1)S(1)} collective-permute-done((bf16[128,768]{1,0:T(8,128)(2,1)S(1)}, bf16[128,768]{1,0:T(8,128)(2,1)S(1)}, u32[]{:S(2)}, u32[]{:S(2)}) %collective-permute-start.26) | collective-permute-done | bytes 196640 | tf_op jit(solution)/shard_map/ppermute | solution.py:871
  90.2 5.8 %ffn.1 = (f32[128,768]{1,0:T(8,128)S(1)}, bf16[128,768]{1,0:T(8,128)(2,1)S(1)}, bf16[128,768]{1,0:T(8,128)(2,1)S(1)}, bf16[128,768]{1,0:T(8,128)(2,1)S(1)}, f32[...) custom-call(s32[2]{0:T(128)S(1)} %pad_add_fusion.places, ...), custom_call_target="tpu_custom_call" | custom-call | flops 3623878656 | bytes 9487872 | tf_op jit(solution)/shard_map/ffn/pallas_call | solution.py:441
  96.1 4.1 %collective-permute-start.28 = (bf16[128,768]{1,0:T(8,128)(2,1)S(1)}, bf16[128,768]{1,0:T(8,128)(2,1)S(1)}, u32[]{:S(2)}, u32[]{:S(2)}) collective-permute-start(bf16[128,768]{1,0:T(8,128)(2,1)S(1)} %get-tuple-element.81), channel_id=1, source_target_pairs={{0,1},{1,0},{2,3},{3,2},{4,5},{5,4},{6,7},{7,6},{8,9},{9,8},{10,11... | collective-permute-start | bytes 589832 | tf_op jit(solution)/shard_map/ppermute | solution.py:871
  100.2 1.7 collective-permute-start.29
  101.9 1.4 collective-permute-start.30
  103.3 2.6 %joined.1 = (f32[128,768]{1,0:T(8,128)S(1)}, bf16[128,768]{1,0:T(8,128)(2,1)S(1)}, bf16[128,768]{1,0:T(8,128)(2,1)S(1)}, bf16[128,768]{1,0:T(8,128)(2,1)S(1)}, f...) custom-call(s32[2]{0:T(128)S(1)} %pad_add_fusion.places, f32[512,384]{1,0:T(8,128)S(1)} %get-tuple-element.84.refs_0_, ...), custom_call_target="tpu_custom_call" | custom-call | flops 905969664 | bytes 7331840 | tf_op jit(solution)/shard_map/joined/pallas_call | solution.py:441
  105.9 3.8 %collective-permute-done.28.refs_8_ = bf16[128,768]{1,0:T(8,128)(2,1)S(1)} collective-permute-done((bf16[128,768]{1,0:T(8,128)(2,1)S(1)}, bf16[128,768]{1,0:T(8,128)(2,1)S(1)}, u32[]{:S(2)}, u32[]{:S(2)}) %collective-permute-start.28) | collective-permute-done | bytes 196640 | tf_op jit(solution)/shard_map/ppermute | solution.py:871
  109.8 7.4 %collective-permute-done.29.refs_9_ = bf16[128,768]{1,0:T(8,128)(2,1)S(1)} collective-permute-done((bf16[128,768]{1,0:T(8,128)(2,1)S(1)}, bf16[128,768]{1,0:T(8,128)(2,1)S(1)}, u32[]{:S(2)}, u32[]{:S(2)}) %collective-permute-start.29) | collective-permute-done | bytes 196640 | tf_op jit(solution)/shard_map/ppermute | solution.py:871
  117.5 3.1 %collective-permute-start.37 = (bf16[128,768]{1,0:T(8,128)(2,1)S(1)}, bf16[128,768]{1,0:T(8,128)(2,1)S(1)}, u32[]{:S(2)}, u32[]{:S(2)}) collective-permute-start(bf16[128,768]{1,0:T(8,128)(2,1)S(1)} %get-tuple-element.99), channel_id=1, source_target_pairs={{0,3},{1,2},{2,1},{3,0},{4,7},{5,6},{6,5},{7,4},{8,11},{9,10},{10,... | collective-permute-start | bytes 589832 | tf_op jit(solution)/shard_map/ppermute | solution.py:871
  122.6 14.8 %collective-permute-done.36.refs_17_ = bf16[128,768]{1,0:T(8,128)(2,1)S(1)} collective-permute-done((bf16[128,768]{1,0:T(8,128)(2,1)S(1)}, bf16[128,768]{1,0:T(8,128)(2,1)S(1)}, u32[]{:S(2)}, u32[]{:S(2)}) %collective-permute-start.36) | collective-permute-done | bytes 196640 | tf_op jit(solution)/shard_map/ppermute | solution.py:871
  140.0 4.1 %collective-permute-start.19 = (bf16[128,768]{1,0:T(8,128)(2,1)S(1)}, bf16[128,768]{1,0:T(8,128)(2,1)S(1)}, u32[]{:S(2)}, u32[]{:S(2)}) collective-permute-start(bf16[128,768]{1,0:T(8,128)(2,1)S(1)} %get-tuple-element.77), channel_id=1, source_target_pairs={{0,8},{4,12},{8,0},{12,4},{16,24},{20,28},{24,16},{28,20},{1,9},{5... | collective-permute-start | bytes 589832 | tf_op jit(solution)/shard_map/ppermute | solution.py:868
  144.0 1.3 collective-permute-done.51
  145.4 2.2 collective-permute-done.50
  148.9 3.6 %collective-permute-start.55 = (bf16[96,768]{1,0:T(8,128)(2,1)S(1)}, bf16[96,768]{1,0:T(8,128)(2,1)S(1)}, u32[]{:S(2)}, u32[]{:S(2)}) collective-permute-start(bf16[96,768]{1,0:T(8,128)(2,1)S(1)} %add_convert_fusion), channel_id=1, source_target_pairs={{0,24},{4,28},{9,17},{13,21},{18,10},{22,14},{27,3},{31,7}} | collective-permute-start | bytes 442376 | tf_op jit(solution)/shard_map/ppermute | solution.py:874
  152.6 2.7 %collective-permute-done.20.refs_5_ = bf16[128,768]{1,0:T(8,128)(2,1)S(1)} collective-permute-done((bf16[128,768]{1,0:T(8,128)(2,1)S(1)}, bf16[128,768]{1,0:T(8,128)(2,1)S(1)}, u32[]{:S(2)}, u32[]{:S(2)}) %collective-permute-start.20) | collective-permute-done | bytes 196640 | tf_op jit(solution)/shard_map/ppermute | solution.py:868
  158.7 1.9 collective-permute-start.39
  161.3 2.5 %collective-permute-start.41 = (bf16[112,576]{1,0:T(8,128)(2,1)S(1)}, bf16[112,576]{1,0:T(8,128)(2,1)S(1)}, u32[]{:S(2)}, u32[]{:S(2)}) collective-permute-start(bf16[112,576]{1,0:T(8,128)(2,1)S(1)} %get-tuple-element.107), channel_id=1, source_target_pairs={{0,3},{1,2},{2,1},{3,0},{4,7},{5,6},{6,5},{7,4},{8,11},{9,10},{10,... | collective-permute-start | bytes 387080 | tf_op jit(solution)/shard_map/ppermute | solution.py:871
  166.0 2.1 collective-permute-start.33
  168.3 2.9 %collective-permute-done.40.b = bf16[112,576]{1,0:T(8,128)(2,1)S(1)} collective-permute-done((bf16[112,576]{1,0:T(8,128)(2,1)S(1)}, bf16[112,576]{1,0:T(8,128)(2,1)S(1)}, u32[]{:S(2)}, u32[]{:S(2)}) %collective-permute-start.40) | collective-permute-done | bytes 129056 | tf_op jit(solution)/shard_map/ppermute | solution.py:871
  171.2 2.8 %collective-permute-start.59 = (bf16[192,768]{1,0:T(8,128)(2,1)S(1)}, bf16[192,768]{1,0:T(8,128)(2,1)S(1)}, u32[]{:S(2)}, u32[]{:S(2)}) collective-permute-start(bf16[192,768]{1,0:T(8,128)(2,1)S(1)} %get-tuple-element.117), channel_id=1, source_target_pairs={{0,16},{4,20},{8,24},{12,28},{16,0},{20,4},{24,8},{28,12},{1,17},{... | collective-permute-start | bytes 884744 | tf_op jit(solution)/shard_map/ppermute | solution.py:868
  176.0 10.6 %collective-permute-done.59.b = bf16[192,768]{1,0:T(8,128)(2,1)S(1)} collective-permute-done((bf16[192,768]{1,0:T(8,128)(2,1)S(1)}, bf16[192,768]{1,0:T(8,128)(2,1)S(1)}, u32[]{:S(2)}, u32[]{:S(2)}) %collective-permute-start.59) | collective-permute-done | bytes 294944 | tf_op jit(solution)/shard_map/ppermute | solution.py:868
  190.1 1.7 collective-permute-start.61
  192.7 1.6 collective-permute-start.63
  194.3 1.4 collective-permute-start.44
  195.7 11.7 %collective-permute-done.44.refs_3_ = bf16[112,576]{1,0:T(8,128)(2,1)} collective-permute-done((bf16[112,576]{1,0:T(8,128)(2,1)S(1)}, bf16[112,576]{1,0:T(8,128)(2,1)}, u32[]{:S(2)}, u32[]{:S(2)}) %collective-permute-start.44) | collective-permute-done | bytes 129056 | tf_op jit(solution)/shard_map/ppermute | solution.py:868
  220.1 1.9 token_.1
  224.0 2.9 %qkv_finish.1 = (f32[192,2304]{1,0:T(8,128)}, f32[8,192]{1,0:T(8,128)S(1)}, f32[1,576]{1,0:T(1,128)S(1)}, f32[1,768]{1,0:T(1,128)S(1)}) custom-call(s32[2]{0:T(128)S(1)} %pad_add_fusion.places, bf16[112,576]{1,0:T(8,128)(2,1)S(1)} %qkv_sum.1.refs_0_, bf16[112,576]{1,0:T(8,128)(2,1)S(1)} %copy-done.27, bf16[112,576]{1,0:T(8,128)(2,1)} %collective-permute-done.43.refs_2_, ...), custom_call_target="tpu_custom_call" | custom-call | bytes 2813184 | tf_op jit(solution)/shard_map/qkv_finish/pallas_call | solution.py:441
  228.7 3.2 %ffn_spread.1 = (f32[768,768]{1,0:T(8,128)}, f32[768,768]{1,0:T(8,128)}) custom-call(s32[2]{0:T(128)S(1)} %pad_add_fusion.places, bf16[192,768]{1,0:T(8,128)(2,1)S(1)} %ffn_sum.1.refs_0_, bf16[192,768]{1,0:T(8,128)(2,1)S(1)} %collective-permute-done.61.refs_1_, bf16[192,768]{1,0:T(8,128)(2,1)S(1)} %collective-permute-done.62.refs_2_, ...), custom_call_target="tpu_custom_call" | custom-call | bytes 7077888 | tf_op jit(solution)/shard_map/ffn_spread/pallas_call | solution.py:441
  (196 shorter events, 47.5 us)
Async XLA Ops:
  6.9 13.8 %collective-permute-start = (bf16[112,576]{1,0:T(8,128)(2,1)S(1)}, bf16[112,576]{1,0:T(8,128)(2,1)S(1)}, u32[]{:S(2)}, u32[]{:S(2)}) collective-permute-start(bf16[112,576]{1,0:T(8,128)(2,1)S(1)} %fusion.2.p0.refs_8_), channel_id=1, source_target_pairs={{0,1},{1,0},{2,3},{3,2},{4,5},{5,4},{6,7},{7,6},{8,9},{9,8},{10,11... | collective-permute-start | bytes 387080 | tf_op jit(solution)/shard_map/ppermute | solution.py:871
  10.0 13.7 %collective-permute-start.1 = (bf16[112,576]{1,0:T(8,128)(2,1)S(1)}, bf16[112,576]{1,0:T(8,128)(2,1)S(1)}, u32[]{:S(2)}, u32[]{:S(2)}) collective-permute-start(bf16[112,576]{1,0:T(8,128)(2,1)S(1)} %fusion.2.p0.refs_8_), channel_id=1, source_target_pairs={{0,2},{1,3},{2,0},{3,1},{4,6},{5,7},{6,4},{7,5},{8,10},{9,11},{10,... | collective-permute-start | bytes 387080 | tf_op jit(solution)/shard_map/ppermute | solution.py:871
  12.6 12.6 %collective-permute-start.2 = (bf16[112,576]{1,0:T(8,128)(2,1)S(1)}, bf16[112,576]{1,0:T(8,128)(2,1)S(1)}, u32[]{:S(2)}, u32[]{:S(2)}) collective-permute-start(bf16[112,576]{1,0:T(8,128)(2,1)S(1)} %fusion.2.p0.refs_8_), channel_id=1, source_target_pairs={{0,3},{1,2},{2,1},{3,0},{4,7},{5,6},{6,5},{7,4},{8,11},{9,10},{10,... | collective-permute-start | bytes 387080 | tf_op jit(solution)/shard_map/ppermute | solution.py:871
  12.6 21.0 %collective-permute-start.3 = (bf16[128,768]{1,0:T(8,128)(2,1)}, bf16[128,768]{1,0:T(8,128)(2,1)S(1)}, u32[]{:S(2)}, u32[]{:S(2)}) collective-permute-start(bf16[128,768]{1,0:T(8,128)(2,1)} %bitcast.11), channel_id=1, source_target_pairs={{0,8},{4,12},{8,0},{12,4},{16,24},{20,28},{24,16},{28,20},{1,9},{5... | collective-permute-start | bytes 589832 | tf_op jit(solution)/shard_map/ppermute | solution.py:868
  15.2 12.8 %collective-permute-start.15 = (bf16[96,768]{1,0:T(8,128)(2,1)S(1)}, bf16[96,768]{1,0:T(8,128)(2,1)S(1)}, u32[]{:S(2)}, u32[]{:S(2)}) collective-permute-start(bf16[96,768]{1,0:T(8,128)(2,1)S(1)} %constant_dynamic-slice_fusion), channel_id=1, source_target_pairs={{0,3},{4,7},{9,10},{13,14},{18,17},{22,21},{27,24},{31,28}} | collective-permute-start | bytes 442376 | tf_op jit(solution)/shard_map/ppermute | solution.py:874
  20.7 10.7 %collective-permute-start.13 = (bf16[96,768]{1,0:T(8,128)(2,1)S(1)}, bf16[96,768]{1,0:T(8,128)(2,1)S(1)}, u32[]{:S(2)}, u32[]{:S(2)}) collective-permute-start(bf16[96,768]{1,0:T(8,128)(2,1)S(1)} %constant_dynamic-slice_fusion), channel_id=1, source_target_pairs={{0,1},{4,5},{9,8},{13,12},{18,19},{22,23},{27,26},{31,30}} | collective-permute-start | bytes 442376 | tf_op jit(solution)/shard_map/ppermute | solution.py:874
  26.6 12.2 %collective-permute-start.4 = (bf16[128,768]{1,0:T(8,128)(2,1)}, bf16[128,768]{1,0:T(8,128)(2,1)S(1)}, u32[]{:S(2)}, u32[]{:S(2)}) collective-permute-start(bf16[128,768]{1,0:T(8,128)(2,1)} %bitcast.12), channel_id=1, source_target_pairs={{0,16},{4,20},{8,24},{12,28},{16,0},{20,4},{24,8},{28,12},{1,17},{... | collective-permute-start | bytes 589832 | tf_op jit(solution)/shard_map/ppermute | solution.py:868
  28.0 10.8 %collective-permute-start.5 = (bf16[128,768]{1,0:T(8,128)(2,1)}, bf16[128,768]{1,0:T(8,128)(2,1)S(1)}, u32[]{:S(2)}, u32[]{:S(2)}) collective-permute-start(bf16[128,768]{1,0:T(8,128)(2,1)} %bitcast.13), channel_id=1, source_target_pairs={{0,24},{4,28},{8,16},{12,20},{16,8},{20,12},{24,0},{28,4},{1,25},{... | collective-permute-start | bytes 589832 | tf_op jit(solution)/shard_map/ppermute | solution.py:868
  31.4 10.8 %collective-permute-start.6 = (bf16[128,768]{1,0:T(8,128)(2,1)}, bf16[128,768]{1,0:T(8,128)(2,1)S(1)}, u32[]{:S(2)}, u32[]{:S(2)}) collective-permute-start(bf16[128,768]{1,0:T(8,128)(2,1)} %bitcast.21), channel_id=1, source_target_pairs={{0,8},{4,12},{8,0},{12,4},{16,24},{20,28},{24,16},{28,20},{1,9},{5... | collective-permute-start | bytes 589832 | tf_op jit(solution)/shard_map/ppermute | solution.py:868
  32.1 14.3 %collective-permute-start.7 = (bf16[128,768]{1,0:T(8,128)(2,1)}, bf16[128,768]{1,0:T(8,128)(2,1)S(1)}, u32[]{:S(2)}, u32[]{:S(2)}) collective-permute-start(bf16[128,768]{1,0:T(8,128)(2,1)} %bitcast.22), channel_id=1, source_target_pairs={{0,16},{4,20},{8,24},{12,28},{16,0},{20,4},{24,8},{28,12},{1,17},{... | collective-permute-start | bytes 589832 | tf_op jit(solution)/shard_map/ppermute | solution.py:868
  33.5 13.7 %collective-permute-start.8 = (bf16[128,768]{1,0:T(8,128)(2,1)}, bf16[128,768]{1,0:T(8,128)(2,1)S(1)}, u32[]{:S(2)}, u32[]{:S(2)}) collective-permute-start(bf16[128,768]{1,0:T(8,128)(2,1)} %bitcast.23), channel_id=1, source_target_pairs={{0,24},{4,28},{8,16},{12,20},{16,8},{20,12},{24,0},{28,4},{1,25},{... | collective-permute-start | bytes 589832 | tf_op jit(solution)/shard_map/ppermute | solution.py:868
  38.8 14.7 %collective-permute-start.16 = (bf16[96,768]{1,0:T(8,128)(2,1)S(1)}, bf16[96,768]{1,0:T(8,128)(2,1)S(1)}, u32[]{:S(2)}, u32[]{:S(2)}) collective-permute-start(bf16[96,768]{1,0:T(8,128)(2,1)S(1)} %add_select_fusion.1.refs_18_), channel_id=1, source_target_pairs={{0,4},{4,0},{8,12},{12,8},{16,20},{20,16},{24,28},{28,24},{1,5},{5... | collective-permute-start | bytes 442376 | tf_op jit(solution)/shard_map/ppermute | solution.py:868
  38.8 14.7 %collective-permute-start.10 = (bf16[112,576]{1,0:T(8,128)(2,1)S(1)}, bf16[112,576]{1,0:T(8,128)(2,1)S(1)}, u32[]{:S(2)}, u32[]{:S(2)}) collective-permute-start(bf16[112,576]{1,0:T(8,128)(2,1)S(1)} %collective-permute-done.p1.refs_9_), channel_id=1, source_target_pairs={{0,4},{4,0},{8,12},{12,8},{16,20},{20,16},{24,28},{28,24},{1,5},{5... | collective-permute-start | bytes 387080 | tf_op jit(solution)/shard_map/ppermute | solution.py:868
  42.2 11.2 %collective-permute-start.11 = (bf16[112,576]{1,0:T(8,128)(2,1)S(1)}, bf16[112,576]{1,0:T(8,128)(2,1)S(1)}, u32[]{:S(2)}, u32[]{:S(2)}) collective-permute-start(bf16[112,576]{1,0:T(8,128)(2,1)S(1)} %collective-permute-done.1.p2.refs_10_), channel_id=1, source_target_pairs={{0,4},{4,0},{8,12},{12,8},{16,20},{20,16},{24,28},{28,24},{1,5},{5... | collective-permute-start | bytes 387080 | tf_op jit(solution)/shard_map/ppermute | solution.py:868
  47.3 12.3 %collective-permute-start.22 = (bf16[128,768]{1,0:T(8,128)(2,1)S(1)}, bf16[128,768]{1,0:T(8,128)(2,1)S(1)}, u32[]{:S(2)}, u32[]{:S(2)}) collective-permute-start(bf16[128,768]{1,0:T(8,128)(2,1)S(1)} %bitcast.14), channel_id=1, source_target_pairs={{0,1},{1,0},{2,3},{3,2},{4,5},{5,4},{6,7},{7,6},{8,9},{9,8},{10,11... | collective-permute-start | bytes 589832 | tf_op jit(solution)/shard_map/ppermute | solution.py:871
  56.2 17.1 %collective-permute-start.23 = (bf16[128,768]{1,0:T(8,128)(2,1)S(1)}, bf16[128,768]{1,0:T(8,128)(2,1)S(1)}, u32[]{:S(2)}, u32[]{:S(2)}) collective-permute-start(bf16[128,768]{1,0:T(8,128)(2,1)S(1)} %bitcast.16), channel_id=1, source_target_pairs={{0,2},{1,3},{2,0},{3,1},{4,6},{5,7},{6,4},{7,5},{8,10},{9,11},{10,... | collective-permute-start | bytes 589832 | tf_op jit(solution)/shard_map/ppermute | solution.py:871
  58.6 14.8 %collective-permute-start.24 = (bf16[128,768]{1,0:T(8,128)(2,1)S(1)}, bf16[128,768]{1,0:T(8,128)(2,1)S(1)}, u32[]{:S(2)}, u32[]{:S(2)}) collective-permute-start(bf16[128,768]{1,0:T(8,128)(2,1)S(1)} %bitcast.17), channel_id=1, source_target_pairs={{0,3},{1,2},{2,1},{3,0},{4,7},{5,6},{6,5},{7,4},{8,11},{9,10},{10,... | collective-permute-start | bytes 589832 | tf_op jit(solution)/shard_map/ppermute | solution.py:871
  59.6 13.7 %collective-permute-start.25 = (bf16[128,768]{1,0:T(8,128)(2,1)S(1)}, bf16[128,768]{1,0:T(8,128)(2,1)S(1)}, u32[]{:S(2)}, u32[]{:S(2)}) collective-permute-start(bf16[128,768]{1,0:T(8,128)(2,1)S(1)} %bitcast.25), channel_id=1, source_target_pairs={{0,1},{1,0},{2,3},{3,2},{4,5},{5,4},{6,7},{7,6},{8,9},{9,8},{10,11... | collective-permute-start | bytes 589832 | tf_op jit(solution)/shard_map/ppermute | solution.py:871
  60.8 29.4 %collective-permute-start.26 = (bf16[128,768]{1,0:T(8,128)(2,1)S(1)}, bf16[128,768]{1,0:T(8,128)(2,1)S(1)}, u32[]{:S(2)}, u32[]{:S(2)}) collective-permute-start(bf16[128,768]{1,0:T(8,128)(2,1)S(1)} %bitcast.26), channel_id=1, source_target_pairs={{0,2},{1,3},{2,0},{3,1},{4,6},{5,7},{6,4},{7,5},{8,10},{9,11},{10,... | collective-permute-start | bytes 589832 | tf_op jit(solution)/shard_map/ppermute | solution.py:871
  63.1 27.1 %collective-permute-start.27 = (bf16[128,768]{1,0:T(8,128)(2,1)S(1)}, bf16[128,768]{1,0:T(8,128)(2,1)S(1)}, u32[]{:S(2)}, u32[]{:S(2)}) collective-permute-start(bf16[128,768]{1,0:T(8,128)(2,1)S(1)} %bitcast.27), channel_id=1, source_target_pairs={{0,3},{1,2},{2,1},{3,0},{4,7},{5,6},{6,5},{7,4},{8,11},{9,10},{10,... | collective-permute-start | bytes 589832 | tf_op jit(solution)/shard_map/ppermute | solution.py:871
  73.4 30.0 %collective-permute-start.31 = (bf16[512,384]{1,0:T(8,128)(2,1)S(1)}, bf16[512,384]{1,0:T(8,128)(2,1)S(1)}, u32[]{:S(2)}, u32[]{:S(2)}) collective-permute-start(bf16[512,384]{1,0:T(8,128)(2,1)S(1)} %get-tuple-element.86), channel_id=1, source_target_pairs={{0,4},{4,0},{8,12},{12,8},{16,20},{20,16},{24,28},{28,24},{1,5},{5... | collective-permute-start | bytes 1179656 | tf_op jit(solution)/shard_map/ppermute | solution.py:868
  96.0 65.4 %collective-permute-start.57 = (bf16[4,192,768]{2,1,0:T(8,128)(2,1)S(1)}, bf16[4,192,768]{2,1,0:T(8,128)(2,1)S(1)}, u32[]{:S(2)}, u32[]{:S(2)}) collective-permute-start(bf16[4,192,768]{2,1,0:T(8,128)(2,1)S(1)} %get-tuple-element.114), channel_id=1, source_target_pairs={{0,4},{4,0},{8,12},{12,8},{16,20},{20,16},{24,28},{28,24},{1,5},{5... | collective-permute-start | bytes 3538952 | tf_op jit(solution)/shard_map/ppermute | solution.py:868
  96.1 13.7 %collective-permute-start.28 = (bf16[128,768]{1,0:T(8,128)(2,1)S(1)}, bf16[128,768]{1,0:T(8,128)(2,1)S(1)}, u32[]{:S(2)}, u32[]{:S(2)}) collective-permute-start(bf16[128,768]{1,0:T(8,128)(2,1)S(1)} %get-tuple-element.81), channel_id=1, source_target_pairs={{0,1},{1,0},{2,3},{3,2},{4,5},{5,4},{6,7},{7,6},{8,9},{9,8},{10,11... | collective-permute-start | bytes 589832 | tf_op jit(solution)/shard_map/ppermute | solution.py:871
  100.2 17.0 %collective-permute-start.29 = (bf16[128,768]{1,0:T(8,128)(2,1)S(1)}, bf16[128,768]{1,0:T(8,128)(2,1)S(1)}, u32[]{:S(2)}, u32[]{:S(2)}) collective-permute-start(bf16[128,768]{1,0:T(8,128)(2,1)S(1)} %get-tuple-element.82), channel_id=1, source_target_pairs={{0,2},{1,3},{2,0},{3,1},{4,6},{5,7},{6,4},{7,5},{8,10},{9,11},{10,... | collective-permute-start | bytes 589832 | tf_op jit(solution)/shard_map/ppermute | solution.py:871
  101.9 15.6 %collective-permute-start.30 = (bf16[128,768]{1,0:T(8,128)(2,1)S(1)}, bf16[128,768]{1,0:T(8,128)(2,1)S(1)}, u32[]{:S(2)}, u32[]{:S(2)}) collective-permute-start(bf16[128,768]{1,0:T(8,128)(2,1)S(1)} %get-tuple-element.83), channel_id=1, source_target_pairs={{0,3},{1,2},{2,1},{3,0},{4,7},{5,6},{6,5},{7,4},{8,11},{9,10},{10,... | collective-permute-start | bytes 589832 | tf_op jit(solution)/shard_map/ppermute | solution.py:871
  103.3 17.3 %collective-permute-start.49 = (bf16[96,768]{1,0:T(8,128)(2,1)S(1)}, bf16[96,768]{1,0:T(8,128)(2,1)S(1)}, u32[]{:S(2)}, u32[]{:S(2)}) collective-permute-start(bf16[96,768]{1,0:T(8,128)(2,1)S(1)} %get-tuple-element.112), channel_id=1, source_target_pairs={{0,4},{4,0},{8,12},{12,8},{16,20},{20,16},{24,28},{28,24},{1,5},{5... | collective-permute-start | bytes 442376 | tf_op jit(solution)/shard_map/ppermute | solution.py:868
  109.8 11.5 %collective-permute-start.35 = (bf16[128,768]{1,0:T(8,128)(2,1)S(1)}, bf16[128,768]{1,0:T(8,128)(2,1)S(1)}, u32[]{:S(2)}, u32[]{:S(2)}) collective-permute-start(bf16[128,768]{1,0:T(8,128)(2,1)S(1)} %get-tuple-element.97), channel_id=1, source_target_pairs={{0,1},{1,0},{2,3},{3,2},{4,5},{5,4},{6,7},{7,6},{8,9},{9,8},{10,11... | collective-permute-start | bytes 589832 | tf_op jit(solution)/shard_map/ppermute | solution.py:871
  117.2 20.2 %collective-permute-start.36 = (bf16[128,768]{1,0:T(8,128)(2,1)S(1)}, bf16[128,768]{1,0:T(8,128)(2,1)S(1)}, u32[]{:S(2)}, u32[]{:S(2)}) collective-permute-start(bf16[128,768]{1,0:T(8,128)(2,1)S(1)} %get-tuple-element.98), channel_id=1, source_target_pairs={{0,2},{1,3},{2,0},{3,1},{4,6},{5,7},{6,4},{7,5},{8,10},{9,11},{10,... | collective-permute-start | bytes 589832 | tf_op jit(solution)/shard_map/ppermute | solution.py:871
  117.5 21.1 %collective-permute-start.37 = (bf16[128,768]{1,0:T(8,128)(2,1)S(1)}, bf16[128,768]{1,0:T(8,128)(2,1)S(1)}, u32[]{:S(2)}, u32[]{:S(2)}) collective-permute-start(bf16[128,768]{1,0:T(8,128)(2,1)S(1)} %get-tuple-element.99), channel_id=1, source_target_pairs={{0,3},{1,2},{2,1},{3,0},{4,7},{5,6},{6,5},{7,4},{8,11},{9,10},{10,... | collective-permute-start | bytes 589832 | tf_op jit(solution)/shard_map/ppermute | solution.py:871
  120.6 37.3 %collective-permute-start.38 = (bf16[4,112,576]{2,1,0:T(8,128)(2,1)S(1)}, bf16[4,112,576]{2,1,0:T(8,128)(2,1)S(1)}, u32[]{:S(2)}, u32[]{:S(2)}) collective-permute-start(bf16[4,112,576]{2,1,0:T(8,128)(2,1)S(1)} %get-tuple-element.103), channel_id=1, source_target_pairs={{0,4},{4,0},{8,12},{12,8},{16,20},{20,16},{24,28},{28,24},{1,5},{5... | collective-permute-start | bytes 1548296 | tf_op jit(solution)/shard_map/ppermute | solution.py:868
  121.3 18.7 %collective-permute-start.52 = (bf16[96,768]{1,0:T(8,128)(2,1)S(1)}, bf16[96,768]{1,0:T(8,128)(2,1)S(1)}, u32[]{:S(2)}, u32[]{:S(2)}) collective-permute-start(bf16[96,768]{1,0:T(8,128)(2,1)S(1)} %add_convert_fusion.1), channel_id=1, source_target_pairs={{3,0},{7,4},{10,9},{14,13},{17,18},{21,22},{24,27},{28,31}} | collective-permute-start | bytes 442376 | tf_op jit(solution)/shard_map/ppermute | solution.py:874
  145.4 9.9 %collective-permute-start.20 = (bf16[128,768]{1,0:T(8,128)(2,1)S(1)}, bf16[128,768]{1,0:T(8,128)(2,1)S(1)}, u32[]{:S(2)}, u32[]{:S(2)}) collective-permute-start(bf16[128,768]{1,0:T(8,128)(2,1)S(1)} %get-tuple-element.78), channel_id=1, source_target_pairs={{0,16},{4,20},{8,24},{12,28},{16,0},{20,4},{24,8},{28,12},{1,17},{... | collective-permute-start | bytes 589832 | tf_op jit(solution)/shard_map/ppermute | solution.py:868
  148.9 9.8 %collective-permute-start.55 = (bf16[96,768]{1,0:T(8,128)(2,1)S(1)}, bf16[96,768]{1,0:T(8,128)(2,1)S(1)}, u32[]{:S(2)}, u32[]{:S(2)}) collective-permute-start(bf16[96,768]{1,0:T(8,128)(2,1)S(1)} %add_convert_fusion), channel_id=1, source_target_pairs={{0,24},{4,28},{9,17},{13,21},{18,10},{22,14},{27,3},{31,7}} | collective-permute-start | bytes 442376 | tf_op jit(solution)/shard_map/ppermute | solution.py:874
  160.6 10.6 %collective-permute-start.40 = (bf16[112,576]{1,0:T(8,128)(2,1)S(1)}, bf16[112,576]{1,0:T(8,128)(2,1)S(1)}, u32[]{:S(2)}, u32[]{:S(2)}) collective-permute-start(bf16[112,576]{1,0:T(8,128)(2,1)S(1)} %get-tuple-element.106), channel_id=1, source_target_pairs={{0,2},{1,3},{2,0},{3,1},{4,6},{5,7},{6,4},{7,5},{8,10},{9,11},{10,... | collective-permute-start | bytes 387080 | tf_op jit(solution)/shard_map/ppermute | solution.py:871
  161.3 12.7 %collective-permute-start.41 = (bf16[112,576]{1,0:T(8,128)(2,1)S(1)}, bf16[112,576]{1,0:T(8,128)(2,1)S(1)}, u32[]{:S(2)}, u32[]{:S(2)}) collective-permute-start(bf16[112,576]{1,0:T(8,128)(2,1)S(1)} %get-tuple-element.107), channel_id=1, source_target_pairs={{0,3},{1,2},{2,1},{3,0},{4,7},{5,6},{6,5},{7,4},{8,11},{9,10},{10,... | collective-permute-start | bytes 387080 | tf_op jit(solution)/shard_map/ppermute | solution.py:871
  164.7 10.6 %collective-permute-start.58 = (bf16[192,768]{1,0:T(8,128)(2,1)S(1)}, bf16[192,768]{1,0:T(8,128)(2,1)S(1)}, u32[]{:S(2)}, u32[]{:S(2)}) collective-permute-start(bf16[192,768]{1,0:T(8,128)(2,1)S(1)} %get-tuple-element.116), channel_id=1, source_target_pairs={{0,8},{4,12},{8,0},{12,4},{16,24},{20,28},{24,16},{28,20},{1,9},{5... | collective-permute-start | bytes 884744 | tf_op jit(solution)/shard_map/ppermute | solution.py:868
  166.0 23.4 %collective-permute-start.33 = (bf16[128,768]{1,0:T(8,128)(2,1)S(1)}, bf16[128,768]{1,0:T(8,128)(2,1)S(1)}, u32[]{:S(2)}, u32[]{:S(2)}) collective-permute-start(bf16[128,768]{1,0:T(8,128)(2,1)S(1)} %get-tuple-element.94), channel_id=1, source_target_pairs={{0,16},{4,20},{8,24},{12,28},{16,0},{20,4},{24,8},{28,12},{1,17},{... | collective-permute-start | bytes 589832 | tf_op jit(solution)/shard_map/ppermute | solution.py:868
  168.1 23.6 %collective-permute-start.34 = (bf16[128,768]{1,0:T(8,128)(2,1)S(1)}, bf16[128,768]{1,0:T(8,128)(2,1)S(1)}, u32[]{:S(2)}, u32[]{:S(2)}) collective-permute-start(bf16[128,768]{1,0:T(8,128)(2,1)S(1)} %get-tuple-element.95), channel_id=1, source_target_pairs={{0,24},{4,28},{8,16},{12,20},{16,8},{20,12},{24,0},{28,4},{1,25},{... | collective-permute-start | bytes 589832 | tf_op jit(solution)/shard_map/ppermute | solution.py:868
  171.2 15.4 %collective-permute-start.59 = (bf16[192,768]{1,0:T(8,128)(2,1)S(1)}, bf16[192,768]{1,0:T(8,128)(2,1)S(1)}, u32[]{:S(2)}, u32[]{:S(2)}) collective-permute-start(bf16[192,768]{1,0:T(8,128)(2,1)S(1)} %get-tuple-element.117), channel_id=1, source_target_pairs={{0,16},{4,20},{8,24},{12,28},{16,0},{20,4},{24,8},{28,12},{1,17},{... | collective-permute-start | bytes 884744 | tf_op jit(solution)/shard_map/ppermute | solution.py:868
  174.1 13.4 %collective-permute-start.60 = (bf16[192,768]{1,0:T(8,128)(2,1)S(1)}, bf16[192,768]{1,0:T(8,128)(2,1)S(1)}, u32[]{:S(2)}, u32[]{:S(2)}) collective-permute-start(bf16[192,768]{1,0:T(8,128)(2,1)S(1)} %get-tuple-element.118), channel_id=1, source_target_pairs={{0,24},{4,28},{8,16},{12,20},{16,8},{20,12},{24,0},{28,4},{1,25},{... | collective-permute-start | bytes 884744 | tf_op jit(solution)/shard_map/ppermute | solution.py:868
  175.3 17.4 %collective-permute-start.56 = (bf16[96,768]{1,0:T(8,128)(2,1)S(1)}, bf16[96,768]{1,0:T(8,128)(2,1)S(1)}, u32[]{:S(2)}, u32[]{:S(2)}) collective-permute-start(bf16[96,768]{1,0:T(8,128)(2,1)S(1)} %add_select_fusion), channel_id=1, source_target_pairs={{0,4},{4,0},{8,12},{12,8},{16,20},{20,16},{24,28},{28,24},{1,5},{5... | collective-permute-start | bytes 442376 | tf_op jit(solution)/shard_map/ppermute | solution.py:868
  190.1 32.4 %collective-permute-start.61 = (bf16[192,768]{1,0:T(8,128)(2,1)S(1)}, bf16[192,768]{1,0:T(8,128)(2,1)S(1)}, u32[]{:S(2)}, u32[]{:S(2)}) collective-permute-start(bf16[192,768]{1,0:T(8,128)(2,1)S(1)} %ffn_sum.1.refs_0_), channel_id=1, source_target_pairs={{0,8},{4,12},{8,0},{12,4},{16,24},{20,28},{24,16},{28,20},{1,9},{5... | collective-permute-start | bytes 884744 | tf_op jit(solution)/shard_map/ppermute | solution.py:868
  192.5 30.1 %collective-permute-start.62 = (bf16[192,768]{1,0:T(8,128)(2,1)S(1)}, bf16[192,768]{1,0:T(8,128)(2,1)S(1)}, u32[]{:S(2)}, u32[]{:S(2)}) collective-permute-start(bf16[192,768]{1,0:T(8,128)(2,1)S(1)} %ffn_sum.1.refs_0_), channel_id=1, source_target_pairs={{0,16},{4,20},{8,24},{12,28},{16,0},{20,4},{24,8},{28,12},{1,17},{... | collective-permute-start | bytes 884744 | tf_op jit(solution)/shard_map/ppermute | solution.py:868
  192.7 30.3 %collective-permute-start.63 = (bf16[192,768]{1,0:T(8,128)(2,1)S(1)}, bf16[192,768]{1,0:T(8,128)(2,1)S(1)}, u32[]{:S(2)}, u32[]{:S(2)}) collective-permute-start(bf16[192,768]{1,0:T(8,128)(2,1)S(1)} %ffn_sum.1.refs_0_), channel_id=1, source_target_pairs={{0,24},{4,28},{8,16},{12,20},{16,8},{20,12},{24,0},{28,4},{1,25},{... | collective-permute-start | bytes 884744 | tf_op jit(solution)/shard_map/ppermute | solution.py:868
  194.3 13.0 %collective-permute-start.44 = (bf16[112,576]{1,0:T(8,128)(2,1)S(1)}, bf16[112,576]{1,0:T(8,128)(2,1)}, u32[]{:S(2)}, u32[]{:S(2)}) collective-permute-start(bf16[112,576]{1,0:T(8,128)(2,1)S(1)} %qkv_sum.1.refs_0_), channel_id=1, source_target_pairs={{0,24},{4,28},{8,16},{12,20},{16,8},{20,12},{24,0},{28,4},{1,25},{... | collective-permute-start | bytes 387080 | tf_op jit(solution)/shard_map/ppermute | solution.py:868
  195.7 12.3 %collective-permute-start.45 = (bf16[112,576]{1,0:T(8,128)(2,1)S(1)}, bf16[112,576]{1,0:T(8,128)(2,1)S(1)}, u32[]{:S(2)}, u32[]{:S(2)}) collective-permute-start(bf16[112,576]{1,0:T(8,128)(2,1)S(1)} %qkv_sum.1.refs_0_), channel_id=1, source_target_pairs={{0,4},{4,0},{8,12},{12,8},{16,20},{20,16},{24,28},{28,24},{1,5},{5... | collective-permute-start | bytes 387080 | tf_op jit(solution)/shard_map/ppermute | solution.py:868
  208.7 13.3 %collective-permute-start.47 = (bf16[112,576]{1,0:T(8,128)(2,1)}, bf16[112,576]{1,0:T(8,128)(2,1)}, u32[]{:S(2)}, u32[]{:S(2)}) collective-permute-start(bf16[112,576]{1,0:T(8,128)(2,1)} %collective-permute-done.43.refs_2_), channel_id=1, source_target_pairs={{0,4},{4,0},{8,12},{12,8},{16,20},{20,16},{24,28},{28,24},{1,5},{5... | collective-permute-start | bytes 387080 | tf_op jit(solution)/shard_map/ppermute | solution.py:868
  209.8 14.1 %collective-permute-start.48 = (bf16[112,576]{1,0:T(8,128)(2,1)}, bf16[112,576]{1,0:T(8,128)(2,1)}, u32[]{:S(2)}, u32[]{:S(2)}) collective-permute-start(bf16[112,576]{1,0:T(8,128)(2,1)} %collective-permute-done.44.refs_3_), channel_id=1, source_target_pairs={{0,4},{4,0},{8,12},{12,8},{16,20},{20,16},{24,28},{28,24},{1,5},{5... | collective-permute-start | bytes 387080 | tf_op jit(solution)/shard_map/ppermute | solution.py:868
  (60 other events, 682.7 us)
